TPU v7x, 512 devices: a whole 4x4x16 slice. The times are simulated.
512 devices in a mesh: grp: 8 (over y, core), dev: 64 (over x, z).
Axes of the slice: x: 4, y: 4, z: 16, core: 2. Of those that a mesh axis runs over, the one named last changes fastest.
Arguments:
- embeddings: bfloat16 [32768, 1024], P(('grp', 'dev')), may hold values from -1000 to 1000, as said below
- labels: int32 [32768], P(('grp', 'dev')), may hold values from 0 to 2047, as said below
- order: int32 [32768], P(('grp', 'dev')), may hold values from 0 to 32767, each once
Outputs:
- max_similarity: float32 [32768], P(('grp', 'dev'))
Inputs may be any that keep to these rules, and one draw needn't show every extreme that they name: On each device, at most 2 rows carry labels with one residue modulo 64; in every draw one residue has exactly 2 rows on every device. `embeddings`: rows of one cluster lie near a common direction; features and rows have unlike scales.
All inputs are finite; a program needn't handle non-finite values.
Results may differ from a plain program's by a relative error of at most 0.00059.
Values may be sent and summed in bfloat16 or wider, within the bound.
No kernel may reach another device: no remote copies, remote signals or barrier semaphores. Data moves between devices by JAX's collectives and lax.ppermute only.
A program may use at most 64 MiB of HBM per device.

v0:
```python
import jax
import jax.numpy as jnp
from jax import lax
from jax.sharding import PartitionSpec as P

EPSILON = 1e-06


def row_maxima(queries, query_labels, query_order, others, other_labels, other_order):
    scores = jnp.einsum("qd,kd->qk", queries, others, preferred_element_type=jnp.float32)
    same_cluster = (query_labels[:, None] == other_labels[None, :]) & (other_labels[None, :] >= 0)
    key_earlier = other_order[None, :] < query_order[:, None]
    return jnp.max(jnp.where(same_cluster & key_earlier, scores, -1.0), axis=1)


def bucket_slots(labels, lane_count):
    target = labels % lane_count
    onehot = (target[:, None] == jnp.arange(lane_count, dtype=jnp.int32)[None, :]).astype(jnp.int32)
    before = jnp.cumsum(onehot, axis=0) - onehot
    return (target, jnp.sum(before * onehot, axis=1))


def body(embeddings, labels, order):
    row_count, feature_width = embeddings.shape
    lane_count = lax.axis_size("dev")
    slot_cap = 2 * row_count // lane_count
    slot_count = lane_count * slot_cap
    floats = embeddings.astype(jnp.float32)
    unit_rows = (
        floats
        * lax.rsqrt(jnp.sum(floats * floats, axis=1, keepdims=True) + feature_width * EPSILON)
    ).astype(jnp.bfloat16)
    target, position = bucket_slots(labels, lane_count)
    placed = target * slot_cap + position
    send_keys = jnp.zeros((slot_count, feature_width), jnp.bfloat16).at[placed].set(unit_rows)
    send_labels = jnp.full((slot_count,), -1, jnp.int32).at[placed].set(labels)
    send_order = jnp.zeros((slot_count,), jnp.int32).at[placed].set(order)
    member_keys, key_labels, key_order = (
        lax.all_to_all(send_keys, "dev", split_axis=0, concat_axis=0, tiled=True),
        lax.all_to_all(send_labels, "dev", split_axis=0, concat_axis=0, tiled=True),
        lax.all_to_all(send_order, "dev", split_axis=0, concat_axis=0, tiled=True),
    )
    initial = jnp.full((slot_count,), -1.0, jnp.float32)
    piece_keys = lax.all_gather(member_keys, "grp", axis=0, tiled=True)
    piece_labels = lax.all_gather(key_labels, "grp", axis=0, tiled=True)
    piece_order = lax.all_gather(key_order, "grp", axis=0, tiled=True)
    found = row_maxima(member_keys, key_labels, key_order, piece_keys, piece_labels, piece_order)
    best_score = jnp.maximum(initial, found)
    returned = lax.all_to_all(best_score, "dev", split_axis=0, concat_axis=0, tiled=True)
    return returned[placed]


def solution(mesh):
    placed = (P(("grp", "dev"), None), P(("grp", "dev")), P(("grp", "dev")))
    return jax.shard_map(
        body, mesh=mesh, in_specs=placed, out_specs=P(("grp", "dev")), check_vma=False
    )
```

profile of v0, /device:TPU:1, one launch (start us, length us, event | category | flops | bytes accessed | tf_op | source)
XLA Modules:
  0.0 145.6 jit_solution(9260794780872003387)
XLA Ops:
  6.5 0.7 and_select_fusion
  7.2 1.0 fusion.1
  8.6 0.7 compare_select_fusion
  9.3 1.4 scatter_custom_fusion.2
  10.8 38.0 %all_to_all.42 = bf16[64,2,1024]{2,1,0:T(2,128)(2,1)S(1)} all-to-all(bf16[64,2,1024]{2,1,0:T(2,128)(2,1)S(1)} %all_to_all.33), channel_id=1, replica_groups=mesh['grp'=8,'dev'=64] {'dev'}, dimensions={0} | all-to-all | bytes 524288 | tf_op jit(solution)/shard_map/all_to_all | solution.py:39
  48.8 0.8 all_to_all.35
  49.6 0.9 scatter_custom_fusion
  50.5 0.7 all_to_all.28
  51.3 7.6 %all-to-all-start = ((s32[64,2,1]{1,2,0:T(1,128)}), s32[64,2,1]{1,2,0:T(1,128)S(1)}, u32[]{:S(2)}, u32[]{:S(2)}) async-start(s32[64,2,1]{1,2,0:T(1,128)} %bitcast), calls=%async_computation | async-start | bytes 65536 | tf_op jit(solution)/shard_map/all_to_all | solution.py:40
  58.9 0.9 scatter_custom_fusion.1
  59.8 0.7 all_to_all.30
  60.5 11.5 %all-to-all-done = s32[64,2,1]{1,2,0:T(1,128)S(1)} async-done(((s32[64,2,1]{1,2,0:T(1,128)}), s32[64,2,1]{1,2,0:T(1,128)S(1)}, u32[]{:S(2)}, u32[]{:S(2)}) %all-to-all-start) | async-done | bytes 544 | tf_op jit(solution)/shard_map/all_to_all | solution.py:40
  72.0 4.5 %all-to-all-start.1 = ((s32[64,2,1]{1,2,0:T(1,128)}), s32[64,2,1]{1,2,0:T(1,128)S(1)}, u32[]{:S(2)}, u32[]{:S(2)}) async-start(s32[64,2,1]{1,2,0:T(1,128)} %bitcast.2), calls=%async_computation.1 | async-start | bytes 65536 | tf_op jit(solution)/shard_map/all_to_all | solution.py:41
  76.7 13.2 %all-to-all-done.1 = s32[64,2,1]{1,2,0:T(1,128)S(1)} async-done(((s32[64,2,1]{1,2,0:T(1,128)}), s32[64,2,1]{1,2,0:T(1,128)S(1)}, u32[]{:S(2)}, u32[]{:S(2)}) %all-to-all-start.1) | async-done | bytes 544 | tf_op jit(solution)/shard_map/all_to_all | solution.py:41
  90.5 0.7 reduce.13
  91.4 0.7 reduce.14
  92.2 14.5 %all-gather = s32[8,1,128]{2,1,0:T(1,128)S(1)} all-gather(s32[1,1,128]{2,1,0:T(1,128)S(1)} %reshape.71), channel_id=1, replica_groups=mesh['grp'=8,'dev'=64] {'grp'}, dimensions={0}, use_global_device_ids=true | all-gather | bytes 4608 | tf_op jit(solution)/shard_map/all_gather | solution.py:45
  106.8 8.0 %all-gather.1 = s32[8,1,128]{2,1,0:T(1,128)S(1)} all-gather(s32[1,1,128]{2,1,0:T(1,128)S(1)} %reshape.73), channel_id=1, replica_groups=mesh['grp'=8,'dev'=64] {'grp'}, dimensions={0}, use_global_device_ids=true | all-gather | bytes 4608 | tf_op jit(solution)/shard_map/all_gather | solution.py:46
  114.8 2.6 %fusion = f32[128]{0:T(128)S(1)} fusion(bf16[128,1024]{1,0:T(8,128)(2,1)} %all_to_all.35, bf16[1024,1024]{1,0:T(8,128)(2,1)} %all-gather.4.cloned.1.call-done, s32[1024]{0:T(1024)S(1)} %bitcast.19, s32[1024]{0:T(1024)S(1)} %bitcast.18, s32[128]{0:T(128)S(1)} %all_to_all.32, s32[128]{0:T(128)S(1)} %eq.33, pred[1024]{0:T(1024)(128)(4,1)S(1)} %broadcast_compare_fusion), kind=kOutput, calls=%fused_computation.5 | convolution fusion | flops 269221760 | bytes 2370048 | tf_op jit(solution)/shard_map/qd,kd->qk/dot_general | solution.py:10
  117.4 0.7 max_broadcast_in_dim.14
  118.2 4.6 %all-to-all-start.3 = ((f32[64,2,1]{1,2,0:T(1,128)}), f32[64,2,1]{1,2,0:T(1,128)S(1)}, u32[]{:S(2)}, u32[]{:S(2)}) async-start(f32[64,2,1]{1,2,0:T(1,128)} %bitcast.4), calls=%async_computation.3 | async-start | bytes 65536 | tf_op jit(solution)/shard_map/all_to_all | solution.py:49
  122.8 13.3 %all-to-all-done.3 = f32[64,2,1]{1,2,0:T(1,128)S(1)} async-done(((f32[64,2,1]{1,2,0:T(1,128)}), f32[64,2,1]{1,2,0:T(1,128)S(1)}, u32[]{:S(2)}, u32[]{:S(2)}) %all-to-all-start.3) | async-done | bytes 544 | tf_op jit(solution)/shard_map/all_to_all | solution.py:49
  136.6 0.7 reduce.15
  137.5 1.3 gather_fusion
  (18 shorter events, 2.2 us)
Async XLA Ops:
  6.5 108.3 %all-gather.4.cloned.1.call-start = ((), (), s32[]{:S(2)}) async-start(), calls=%async_computation.4 | async-start | bytes 2359296 | tf_op jit(solution)/shard_map/all_gather | solution.py:44
  51.3 20.7 %all-to-all-start = ((s32[64,2,1]{1,2,0:T(1,128)}), s32[64,2,1]{1,2,0:T(1,128)S(1)}, u32[]{:S(2)}, u32[]{:S(2)}) async-start(s32[64,2,1]{1,2,0:T(1,128)} %bitcast), calls=%async_computation | async-start | bytes 65536 | tf_op jit(solution)/shard_map/all_to_all | solution.py:40
  72.0 17.8 %all-to-all-start.1 = ((s32[64,2,1]{1,2,0:T(1,128)}), s32[64,2,1]{1,2,0:T(1,128)S(1)}, u32[]{:S(2)}, u32[]{:S(2)}) async-start(s32[64,2,1]{1,2,0:T(1,128)} %bitcast.2), calls=%async_computation.1 | async-start | bytes 65536 | tf_op jit(solution)/shard_map/all_to_all | solution.py:41
  118.2 17.9 %all-to-all-start.3 = ((f32[64,2,1]{1,2,0:T(1,128)}), f32[64,2,1]{1,2,0:T(1,128)S(1)}, u32[]{:S(2)}, u32[]{:S(2)}) async-start(f32[64,2,1]{1,2,0:T(1,128)} %bitcast.4), calls=%async_computation.3 | async-start | bytes 65536 | tf_op jit(solution)/shard_map/all_to_all | solution.py:49
Sparse Core Ops, SparseCore 0:
  49.7 27.8 all-gather.3
where the time goes:
time: 146 us
  blocking collectives  60.5 us (41%)
  waiting for transfers between devices  37.9 us (26%)
  starting transfers between devices  16.7 us (11%)
  between operations  13.5 us (9%)
  local copies, waits for them, and re-layouts  7.96 us (5%)
  other arithmetic  6.32 us (4%)
  matrix products  2.62 us (2%)
    all_to_all x1, blocking collectives, body(): lax.all_to_all(send_keys, 'dev', split_axis=0, concat_axis=0, tiled=True)  38 us
    all_gather x1, blocking collectives, body(): piece_labels = lax.all_gather(key_labels, 'grp', axis=0, tiled=True)  14.5 us
    all_to_all x1, waiting for transfers between devices, body(): lax.all_to_all(best_score, 'dev', split_axis=0, concat_axis=0, tiled=True)  13.3 us
    all_to_all x1, waiting for transfers between devices, body(): lax.all_to_all(send_order, 'dev', split_axis=0, concat_axis=0, tiled=True)  13.2 us
    all_to_all x1, waiting for transfers between devices, body(): lax.all_to_all(send_labels, 'dev', split_axis=0, concat_axis=0, tiled=True)  11.5 us
    all_gather x1, blocking collectives, body(): piece_order = lax.all_gather(key_order, 'grp', axis=0, tiled=True)  8.03 us
    all_to_all x1, starting transfers between devices, body(): lax.all_to_all(send_labels, 'dev', split_axis=0, concat_axis=0, tiled=True)  7.59 us
    all_to_all x1, starting transfers between devices, body(): lax.all_to_all(best_score, 'dev', split_axis=0, concat_axis=0, tiled=True)  4.62 us
  transfers between devices with their start and end apart: 4, of which 3 were waited for; matrix products, arithmetic and copies ran while one was open for 3% of the time, Pallas kernels for 0%

commit v1 on v0

v1 whole, which is shorter than its diff:
```python
import jax
import jax.numpy as jnp
from jax import lax
from jax.experimental import pallas as pl
from jax.experimental.pallas import tpu as pltpu
from jax.sharding import PartitionSpec as P

EPSILON = 1e-06
NX = 4
META = 128
NT = (((1,), (1,)), ((), ()))
VMEM = pl.BlockSpec(memory_space=pltpu.VMEM)


def slots(labels, lanes):
    rows = labels.shape[1]
    target = lax.rem(labels, lanes)
    hit = lax.broadcasted_iota(jnp.int32, (lanes, rows), 0) == target
    earlier = lax.broadcasted_iota(jnp.int32, (rows, rows), 0) < lax.broadcasted_iota(jnp.int32, (rows, rows), 1)
    before = jnp.dot(
        hit.astype(jnp.bfloat16), earlier.astype(jnp.bfloat16), preferred_element_type=jnp.float32
    )
    place = jnp.sum(jnp.where(hit, before, 0.0), axis=0, keepdims=True).astype(jnp.int32)
    return target, hit, place


def pack_kernel(lanes, emb_ref, labels_ref, order_ref, out_ref):
    rows, width = emb_ref.shape
    slot_count = out_ref.shape[0]
    floats = emb_ref[...].astype(jnp.float32)
    scale = lax.rsqrt(jnp.sum(floats * floats, axis=1, keepdims=True) + width * EPSILON)
    unit = (floats * scale).astype(jnp.bfloat16)
    labels = labels_ref[...]
    target, _, place = slots(labels, lanes)
    cap = slot_count // lanes
    here = lax.broadcasted_iota(jnp.int32, (slot_count, rows), 0) == target * cap + place
    out_ref[:, :width] = jnp.dot(
        here.astype(jnp.bfloat16), unit, preferred_element_type=jnp.float32
    ).astype(jnp.bfloat16)

    def column(values):
        return jnp.sum(jnp.where(here, values.astype(jnp.float32), 0.0), axis=1, keepdims=True)

    order = order_ref[...]
    lane = lax.broadcasted_iota(jnp.int32, (slot_count, META), 1)
    meta = jnp.where(lane == 0, column(labels // lanes + 1), 0.0)
    meta = jnp.where(lane == 1, column(order // 256), meta)
    meta = jnp.where(lane == 2, column(lax.rem(order, 256)), meta)
    out_ref[:, width:] = meta.astype(jnp.bfloat16)


def gram_kernel(a_ref, b_ref, c_ref, d_ref, *outs):
    width = a_ref.shape[1] - META
    size = a_ref.shape[0]
    blocks = jnp.concatenate([a_ref[...], b_ref[...], c_ref[...], d_ref[...]], axis=0)
    keys, meta = blocks[:, :width], blocks[:, width:]
    scores = lax.dot_general(keys, keys, NT, preferred_element_type=jnp.float32)
    r = lax.broadcasted_iota(jnp.int32, (8, META), 0)
    c = lax.broadcasted_iota(jnp.int32, (8, META), 1)
    weights = jnp.where((r == 0) & (c == 0) | (r == 1) & (c == 2), 1.0, 0.0)
    weights = jnp.where((r == 1) & (c == 1), 256.0, weights).astype(jnp.bfloat16)
    across = lax.dot_general(weights, meta, NT, preferred_element_type=jnp.float32)
    down = meta[:, :8].astype(jnp.float32)
    label_down = down[:, 0:1]
    order_down = down[:, 1:2] * 256.0 + down[:, 2:3]
    valid = (label_down == across[0:1, :]) & (order_down < across[1:2, :])
    best = jnp.max(jnp.where(valid, scores, -1.0), axis=0, keepdims=True)
    for k, out in enumerate(outs):
        out[...] = best[:, k * size : (k + 1) * size]


def spread_kernel(nz, a_ref, b_ref, c_ref, d_ref, out_ref):
    best = jnp.maximum(jnp.maximum(a_ref[...], b_ref[...]), jnp.maximum(c_ref[...], d_ref[...]))
    lanes, size = out_ref.shape
    cap = size // lanes
    home = lax.broadcasted_iota(jnp.int32, (lanes, size), 0)
    slot = lax.broadcasted_iota(jnp.int32, (lanes, size), 1) // cap
    mine = home == lax.rem(slot, NX) * nz + slot // NX
    out_ref[...] = jnp.where(mine, best, -4.0)


def pick_kernel(returned_ref, labels_ref, out_ref):
    lanes, size = returned_ref.shape
    _, hit, place = slots(labels_ref[...], lanes)
    cap = size // lanes
    lane = lax.rem(lax.broadcasted_iota(jnp.int32, (lanes, size), 1), cap)
    returned = returned_ref[...]
    best = jnp.full(hit.shape, -4.0, jnp.float32)
    for p in range(cap):
        value = jnp.max(jnp.where(lane == p, returned, -4.0), axis=1, keepdims=True)
        best = jnp.where(hit & (place == p), value, best)
    out_ref[...] = jnp.max(best, axis=0, keepdims=True)


def call(kernel, outs, count):
    return pl.pallas_call(
        kernel,
        out_shape=outs,
        in_specs=[VMEM] * count,
        out_specs=jax.tree.map(lambda _: VMEM, outs),
        compiler_params=pltpu.CompilerParams(vmem_limit_bytes=16 * 1024 * 1024),
    )


def body(embeddings, labels, order):
    rows, width = embeddings.shape
    lanes = lax.axis_size("dev")
    groups = lax.axis_size("grp")
    nz = lanes // NX
    cap = 2 * rows // lanes
    slot_count = lanes * cap
    wide = width + META
    labels, order = labels.reshape(1, rows), order.reshape(1, rows)
    along_x = [[x * nz + z for x in range(NX)] for z in range(nz)]
    along_z = [[x * nz + z for z in range(nz)] for x in range(NX)]

    sent = call(
        lambda *refs: pack_kernel(lanes, *refs), jax.ShapeDtypeStruct((slot_count, wide), jnp.bfloat16), 3
    )(embeddings, labels, order)
    sent = lax.all_to_all(
        sent.reshape(NX, nz * cap, wide), "dev", 0, 0, axis_index_groups=along_x, tiled=True
    )
    sent = sent.reshape(NX, nz, cap, wide).transpose(1, 0, 2, 3).reshape(nz, NX * cap, wide)
    sent = lax.all_to_all(sent, "dev", 0, 0, axis_index_groups=along_z, tiled=True)
    block = sent.reshape(slot_count, wide)

    def moves(shift, flip):
        return [(i, (i + shift) % groups ^ flip) for i in range(groups)]

    steps = [moves(groups // 2, 1), moves(2, 0), moves(0, 1)]
    fetched = [lax.ppermute(block, "grp", step) for step in steps]
    partial = call(gram_kernel, [jax.ShapeDtypeStruct((1, slot_count), jnp.float32)] * 4, 4)(block, *fetched)
    back = [
        lax.ppermute(part, "grp", [(j, i) for i, j in step]) for part, step in zip(partial[1:], steps)
    ]
    spread = call(
        lambda *refs: spread_kernel(nz, *refs), jax.ShapeDtypeStruct((lanes, slot_count), jnp.float32), 4
    )(partial[0], *back)
    returned = lax.all_to_all(spread.reshape(lanes, 1, slot_count), "dev", 0, 0, tiled=True)
    best = call(pick_kernel, jax.ShapeDtypeStruct((1, rows), jnp.float32), 2)(
        returned.reshape(lanes, slot_count), labels
    )
    return best.reshape(rows)


def solution(mesh):
    placed = (P(("grp", "dev"), None), P(("grp", "dev")), P(("grp", "dev")))
    return jax.shard_map(
        body, mesh=mesh, in_specs=placed, out_specs=P(("grp", "dev")), check_vma=False
    )
```

time: 146 us -> 100 us (0.68)
  waiting for transfers between devices: 37.9 us -> 12.5 us
  between operations: 13.5 us -> 0.1 us
  starting transfers between devices: 16.7 us -> 24.2 us
  other arithmetic: 6.32 us -> 0 us
  local copies, waits for them, and re-layouts: 7.96 us -> 2 us
  matrix products: 2.62 us -> 0 us
  Pallas kernels: 0 us -> 2.05 us
  blocking collectives: 60.5 us -> 58.5 us
    all_to_all x3 -> x0, waiting for transfers between devices: 37.9 us -> none  [the longest x1 13.3 us: body(): lax.all_to_all(best_score, 'dev', split_axis=0, concat_axis=0, tiled=True)]
    ppermute x0 -> x6, starting transfers between devices: none -> 24.2 us  [the longest x3 17.4 us: body(): fetched = [lax.ppermute(block, 'grp', step) for step in steps]]
    all_gather x2 -> x0, blocking collectives: 22.6 us -> none  [the longest x1 14.5 us: body(): piece_labels = lax.all_gather(key_labels, 'grp', axis=0, tiled=True)]
    all_to_all x1 -> x3, blocking collectives: 38 us -> 58.5 us  [the longest x1 27.9 us: body(): lax.all_to_all(sent, 'dev', 0, 0, axis_index_groups=along_z, tiled=True)]
    all_to_all x3 -> x0, starting transfers between devices: 16.7 us -> none  [the longest x1 7.59 us: body(): lax.all_to_all(send_labels, 'dev', split_axis=0, concat_axis=0, tiled=True)]
    ppermute x0 -> x6, waiting for transfers between devices: none -> 12.5 us  [the longest x3 11.5 us: body(): fetched = [lax.ppermute(block, 'grp', step) for step in steps]]
    all_to_all x8 -> x0, local copies, waits for them, and re-layouts: 3.71 us -> none  [the longest x3 1.39 us: body(): lax.all_to_all(send_order, 'dev', split_axis=0, concat_axis=0, tiled=True)]
    dot_general x1 -> x0, matrix products: 2.62 us -> none  [row_maxima(): jnp.einsum('qd,kd->qk', queries, others, preferred_element_type=jnp.float32)]
  transfers between devices with their start and end apart: 4 -> 6, of which waited for: 3 -> 4; matrix products, arithmetic and copies ran while one was open for 3% -> 0% of each run, Pallas kernels for 0% -> 0%
where the time goes in v1:
time: 100 us; the launch traced here: 99.5 us
  blocking collectives  58.5 us (58%)
  starting transfers between devices  24.2 us (24%)
  waiting for transfers between devices  12.5 us (12%)
  Pallas kernels  2.05 us (2%)
  local copies, waits for them, and re-layouts  2 us (2%)
    all_to_all x1, blocking collectives, body(): lax.all_to_all(sent, 'dev', 0, 0, axis_index_groups=along_z, tiled=True)  27.9 us
    all_to_all x1, blocking collectives, body(): lax.all_to_all(spread.reshape(lanes, 1, slot_count), 'dev', 0, 0, tiled=T...  20.3 us
    ppermute x3, starting transfers between devices, body(): fetched = [lax.ppermute(block, 'grp', step) for step in steps]  17.4 us
    ppermute x3, waiting for transfers between devices, body(): fetched = [lax.ppermute(block, 'grp', step) for step in steps]  11.5 us
    all_to_all x1, blocking collectives, body(): lax.all_to_all(sent.reshape(NX, nz * cap, wide), 'dev', 0, 0, axis_index_...  10.3 us
    ppermute x3, starting transfers between devices, body(): lax.ppermute(part, 'grp', [(j, i) for i, j in step])  6.79 us
  transfers between devices with their start and end apart: 6, of which 4 were waited for; matrix products, arithmetic and copies ran while one was open for 0% of the time, Pallas kernels for 0%

profile of v1, /device:TPU:1, one launch (start us, length us, event | category | flops | bytes accessed | tf_op | source)
XLA Modules:
  0.0 99.5 jit_solution(9562219967382646104)
XLA Ops:
  0.0 0.7 copy-done.1
  0.7 0.0 copy-done.2
  0.7 0.9 copy-done
  1.6 0.3 shard_map.37
  1.9 10.3 %all_to_all.15 = bf16[4,32,1152]{2,1,0:T(8,128)(2,1)S(1)} all-to-all(bf16[4,32,1152]{2,1,0:T(8,128)(2,1)S(1)} %bitcast.12), channel_id=1, replica_groups={{0,16,32,48},{1,17,33,49},{2,18,34,50},{3,19,35,51},{4,20,36,52},{5,21,..., dimensions={0} | all-to-all | bytes 589824 | tf_op jit(solution)/shard_map/all_to_all | solution.py:120
  12.3 0.1 reshape.30
  12.4 0.2 copy.8
  12.6 0.1 reshape.31
  12.7 27.9 %all_to_all.16 = bf16[16,8,1152]{2,1,0:T(8,128)(2,1)S(1)} all-to-all(bf16[16,8,1152]{2,1,0:T(8,128)(2,1)S(1)} %reshape.31), channel_id=1, replica_groups={{0,1,2,3,4,5,6,7,8,9,10,11,12,13,14,15},{16,17,18,19,20,21,22,23,24,25,..., dimensions={0} | all-to-all | bytes 589824 | tf_op jit(solution)/shard_map/all_to_all | solution.py:124
  40.6 9.5 %collective-permute-start.2 = (bf16[128,1152]{1,0:T(8,128)(2,1)S(1)}, bf16[128,1152]{1,0:T(8,128)(2,1)S(1)}, u32[]{:S(2)}, u32[]{:S(2)}) collective-permute-start(bf16[128,1152]{1,0:T(8,128)(2,1)S(1)} %bitcast.13), channel_id=1, source_target_pairs={{0,64},{64,0},{128,192},{192,128},{256,320},{320,256},{384,448},{4... | collective-permute-start | bytes 884744 | tf_op jit(solution)/shard_map/ppermute | solution.py:131
  50.2 3.2 %collective-permute-start.1 = (bf16[128,1152]{1,0:T(8,128)(2,1)S(1)}, bf16[128,1152]{1,0:T(8,128)(2,1)S(1)}, u32[]{:S(2)}, u32[]{:S(2)}) collective-permute-start(bf16[128,1152]{1,0:T(8,128)(2,1)S(1)} %bitcast.14), channel_id=1, source_target_pairs={{0,128},{64,192},{128,256},{192,320},{256,384},{320,448},{384,0},{... | collective-permute-start | bytes 884744 | tf_op jit(solution)/shard_map/ppermute | solution.py:131
  53.4 4.7 %collective-permute-start = (bf16[128,1152]{1,0:T(8,128)(2,1)S(1)}, bf16[128,1152]{1,0:T(8,128)(2,1)S(1)}, u32[]{:S(2)}, u32[]{:S(2)}) collective-permute-start(bf16[128,1152]{1,0:T(8,128)(2,1)S(1)} %bitcast.15), channel_id=1, source_target_pairs={{0,320},{64,256},{128,448},{192,384},{256,64},{320,0},{384,192},{4... | collective-permute-start | bytes 884744 | tf_op jit(solution)/shard_map/ppermute | solution.py:131
  58.1 0.0 collective-permute-done.2.d_ref
  58.1 3.9 %collective-permute-done.1.c_ref = bf16[128,1152]{1,0:T(8,128)(2,1)S(1)} collective-permute-done((bf16[128,1152]{1,0:T(8,128)(2,1)S(1)}, bf16[128,1152]{1,0:T(8,128)(2,1)S(1)}, u32[]{:S(2)}, u32[]{:S(2)}) %collective-permute-start.1) | collective-permute-done | bytes 294944 | tf_op jit(solution)/shard_map/ppermute | solution.py:131
  62.1 7.5 %collective-permute-done.b_ref = bf16[128,1152]{1,0:T(8,128)(2,1)S(1)} collective-permute-done((bf16[128,1152]{1,0:T(8,128)(2,1)S(1)}, bf16[128,1152]{1,0:T(8,128)(2,1)S(1)}, u32[]{:S(2)}, u32[]{:S(2)}) %collective-permute-start) | collective-permute-done | bytes 294944 | tf_op jit(solution)/shard_map/ppermute | solution.py:131
  69.6 1.0 %shard_map.38 = (f32[1,128]{1,0:T(1,128)S(1)}, f32[1,128]{1,0:T(1,128)S(1)}, f32[1,128]{1,0:T(1,128)S(1)}, f32[1,128]{1,0:T(1,128)S(1)}) custom-call(bf16[128,1152]{1,0:T(8,128)(2,1)S(1)} %bitcast.16, bf16[128,1152]{1,0:T(8,128)(2,1)S(1)} %collective-permute-done.b_ref, bf16[128,1152]{1,0:T(8,128)(2,1)S(1)} %collective-permute-done.1.c_ref, ...), custom_call_target="tpu_custom_call" | custom-call | tf_op jit(solution)/shard_map/pallas_call | solution.py:132
  70.6 2.9 %collective-permute-start.3 = (f32[1,128]{1,0:T(1,128)S(1)}, f32[1,128]{1,0:T(1,128)S(1)}, u32[]{:S(2)}, u32[]{:S(2)}) collective-permute-start(f32[1,128]{1,0:T(1,128)S(1)} %get-tuple-element.10), channel_id=1, source_target_pairs={{320,0},{256,64},{448,128},{384,192},{64,256},{0,320},{192,384},{1... | collective-permute-start | bytes 1544 | tf_op jit(solution)/shard_map/ppermute | solution.py:134
  73.6 1.9 %collective-permute-start.4 = (f32[1,128]{1,0:T(1,128)S(1)}, f32[1,128]{1,0:T(1,128)S(1)}, u32[]{:S(2)}, u32[]{:S(2)}) collective-permute-start(f32[1,128]{1,0:T(1,128)S(1)} %get-tuple-element.11), channel_id=1, source_target_pairs={{128,0},{192,64},{256,128},{320,192},{384,256},{448,320},{0,384},{... | collective-permute-start | bytes 1544 | tf_op jit(solution)/shard_map/ppermute | solution.py:134
  75.5 1.9 %collective-permute-start.5 = (f32[1,128]{1,0:T(1,128)S(1)}, f32[1,128]{1,0:T(1,128)S(1)}, u32[]{:S(2)}, u32[]{:S(2)}) collective-permute-start(f32[1,128]{1,0:T(1,128)S(1)} %get-tuple-element.12), channel_id=1, source_target_pairs={{64,0},{0,64},{192,128},{128,192},{320,256},{256,320},{448,384},{3... | collective-permute-start | bytes 1544 | tf_op jit(solution)/shard_map/ppermute | solution.py:134
  77.4 0.0 collective-permute-done.3.refs_1_
  77.4 0.4 collective-permute-done.4.refs_2_
  77.8 0.7 collective-permute-done.5.refs_3_
  78.5 20.3 %all_to_all.17 = f32[64,1,128]{2,1,0:T(1,128)S(1)} all-to-all(f32[64,1,128]{2,1,0:T(1,128)S(1)} %bitcast.17), channel_id=1, replica_groups=mesh['grp'=8,'dev'=64] {'dev'}, dimensions={0} | all-to-all | bytes 65536 | tf_op jit(solution)/shard_map/all_to_all | solution.py:139
  98.8 0.7 shard_map.40
  (4 shorter events, 0.0 us)
Async XLA Ops:
  0.0 0.7 copy-start.1
  0.0 0.7 copy-start.2
  0.7 0.9 copy-start
  40.6 17.5 %collective-permute-start.2 = (bf16[128,1152]{1,0:T(8,128)(2,1)S(1)}, bf16[128,1152]{1,0:T(8,128)(2,1)S(1)}, u32[]{:S(2)}, u32[]{:S(2)}) collective-permute-start(bf16[128,1152]{1,0:T(8,128)(2,1)S(1)} %bitcast.13), channel_id=1, source_target_pairs={{0,64},{64,0},{128,192},{192,128},{256,320},{320,256},{384,448},{4... | collective-permute-start | bytes 884744 | tf_op jit(solution)/shard_map/ppermute | solution.py:131
  50.2 11.9 %collective-permute-start.1 = (bf16[128,1152]{1,0:T(8,128)(2,1)S(1)}, bf16[128,1152]{1,0:T(8,128)(2,1)S(1)}, u32[]{:S(2)}, u32[]{:S(2)}) collective-permute-start(bf16[128,1152]{1,0:T(8,128)(2,1)S(1)} %bitcast.14), channel_id=1, source_target_pairs={{0,128},{64,192},{128,256},{192,320},{256,384},{320,448},{384,0},{... | collective-permute-start | bytes 884744 | tf_op jit(solution)/shard_map/ppermute | solution.py:131
  53.4 16.2 %collective-permute-start = (bf16[128,1152]{1,0:T(8,128)(2,1)S(1)}, bf16[128,1152]{1,0:T(8,128)(2,1)S(1)}, u32[]{:S(2)}, u32[]{:S(2)}) collective-permute-start(bf16[128,1152]{1,0:T(8,128)(2,1)S(1)} %bitcast.15), channel_id=1, source_target_pairs={{0,320},{64,256},{128,448},{192,384},{256,64},{320,0},{384,192},{4... | collective-permute-start | bytes 884744 | tf_op jit(solution)/shard_map/ppermute | solution.py:131
  70.6 6.8 %collective-permute-start.3 = (f32[1,128]{1,0:T(1,128)S(1)}, f32[1,128]{1,0:T(1,128)S(1)}, u32[]{:S(2)}, u32[]{:S(2)}) collective-permute-start(f32[1,128]{1,0:T(1,128)S(1)} %get-tuple-element.10), channel_id=1, source_target_pairs={{320,0},{256,64},{448,128},{384,192},{64,256},{0,320},{192,384},{1... | collective-permute-start | bytes 1544 | tf_op jit(solution)/shard_map/ppermute | solution.py:134
  73.6 4.3 %collective-permute-start.4 = (f32[1,128]{1,0:T(1,128)S(1)}, f32[1,128]{1,0:T(1,128)S(1)}, u32[]{:S(2)}, u32[]{:S(2)}) collective-permute-start(f32[1,128]{1,0:T(1,128)S(1)} %get-tuple-element.11), channel_id=1, source_target_pairs={{128,0},{192,64},{256,128},{320,192},{384,256},{448,320},{0,384},{... | collective-permute-start | bytes 1544 | tf_op jit(solution)/shard_map/ppermute | solution.py:134
  75.5 3.0 %collective-permute-start.5 = (f32[1,128]{1,0:T(1,128)S(1)}, f32[1,128]{1,0:T(1,128)S(1)}, u32[]{:S(2)}, u32[]{:S(2)}) collective-permute-start(f32[1,128]{1,0:T(1,128)S(1)} %get-tuple-element.12), channel_id=1, source_target_pairs={{64,0},{0,64},{192,128},{128,192},{320,256},{256,320},{448,384},{3... | collective-permute-start | bytes 1544 | tf_op jit(solution)/shard_map/ppermute | solution.py:134

commit v2 on v1

v2 whole, which is shorter than its diff:
```python
import jax
import jax.numpy as jnp
from jax import lax
from jax.experimental import pallas as pl
from jax.experimental.pallas import tpu as pltpu
from jax.sharding import Mesh
from jax.sharding import PartitionSpec as P

EPSILON = 1e-06
NX = 4
NY = 4
META = 128
NT = (((1,), (1,)), ((), ()))
VMEM = pl.BlockSpec(memory_space=pltpu.VMEM)


def slots(labels, lanes):
    rows = labels.shape[1]
    target = lax.rem(labels, lanes)
    hit = lax.broadcasted_iota(jnp.int32, (lanes, rows), 0) == target
    earlier = lax.broadcasted_iota(jnp.int32, (rows, rows), 0) < lax.broadcasted_iota(jnp.int32, (rows, rows), 1)
    before = jnp.dot(
        hit.astype(jnp.bfloat16), earlier.astype(jnp.bfloat16), preferred_element_type=jnp.float32
    )
    place = jnp.sum(jnp.where(hit, before, 0.0), axis=0, keepdims=True).astype(jnp.int32)
    return target, hit, place


def pack_kernel(lanes, emb_ref, labels_ref, order_ref, out_ref):
    rows, width = emb_ref.shape
    slot_count = out_ref.shape[0]
    floats = emb_ref[...].astype(jnp.float32)
    scale = lax.rsqrt(jnp.sum(floats * floats, axis=1, keepdims=True) + width * EPSILON)
    unit = (floats * scale).astype(jnp.bfloat16)
    labels = labels_ref[...]
    target, _, place = slots(labels, lanes)
    cap = slot_count // lanes
    here = lax.broadcasted_iota(jnp.int32, (slot_count, rows), 0) == target * cap + place
    out_ref[:, :width] = jnp.dot(
        here.astype(jnp.bfloat16), unit, preferred_element_type=jnp.float32
    ).astype(jnp.bfloat16)

    def column(values):
        return jnp.sum(jnp.where(here, values.astype(jnp.float32), 0.0), axis=1, keepdims=True)

    order = order_ref[...]
    lane = lax.broadcasted_iota(jnp.int32, (slot_count, META), 1)
    meta = jnp.where(lane == 0, column(labels // lanes + 1), 0.0)
    meta = jnp.where(lane == 1, column(order // 256), meta)
    meta = jnp.where(lane == 2, column(lax.rem(order, 256)), meta)
    out_ref[:, width:] = meta.astype(jnp.bfloat16)


def gram_kernel(core_ref, own_ref, other_ref, lane_ref, out_ref):
    width = own_ref.shape[1] - META
    size = own_ref.shape[0]
    dests = out_ref.shape[0] // 2
    core = core_ref[0]
    queries = jnp.concatenate([own_ref[...], other_ref[...]], axis=0)
    members = lane_ref[...]
    scores = lax.dot_general(
        members[:, :width], queries[:, :width], NT, preferred_element_type=jnp.float32
    )
    r = lax.broadcasted_iota(jnp.int32, (8, META), 0)
    c = lax.broadcasted_iota(jnp.int32, (8, META), 1)
    weights = jnp.where((r == 0) & (c == 0) | (r == 1) & (c == 2), 1.0, 0.0)
    weights = jnp.where((r == 1) & (c == 1), 256.0, weights).astype(jnp.bfloat16)
    across = lax.dot_general(weights, queries[:, width:], NT, preferred_element_type=jnp.float32)
    down = members[:, width:].astype(jnp.float32)
    label_down = down[:, 0:1]
    order_down = down[:, 1:2] * 256.0 + down[:, 2:3]
    valid = (label_down == across[0:1, :]) & (order_down < across[1:2, :])
    best = jnp.max(jnp.where(valid, scores, -1.0), axis=0, keepdims=True)
    own, other = best[:, :size], best[:, size:]
    home = lax.broadcasted_iota(jnp.int32, (dests, size), 0)
    slot = lax.broadcasted_iota(jnp.int32, (dests, size), 1) // (size // dests)
    mine = home == slot
    out_ref[:dests, :] = jnp.where(mine, jnp.where(core == 0, own, other), -4.0)
    out_ref[dests:, :] = jnp.where(mine, jnp.where(core == 0, other, own), -4.0)


def pick_kernel(returned_ref, labels_ref, out_ref):
    lanes, size = returned_ref.shape[0] // 2, returned_ref.shape[1]
    _, hit, place = slots(labels_ref[...], lanes)
    cap = size // lanes
    lane = lax.rem(lax.broadcasted_iota(jnp.int32, (lanes, size), 1), cap)
    returned = jnp.maximum(returned_ref[:lanes, :], returned_ref[lanes:, :])
    best = jnp.full(hit.shape, -4.0, jnp.float32)
    for p in range(cap):
        value = jnp.max(jnp.where(lane == p, returned, -4.0), axis=1, keepdims=True)
        best = jnp.where(hit & (place == p), value, best)
    out_ref[...] = jnp.max(best, axis=0, keepdims=True)


def call(kernel, outs, specs):
    return pl.pallas_call(
        kernel,
        out_shape=outs,
        in_specs=specs,
        out_specs=jax.tree.map(lambda _: VMEM, outs),
        compiler_params=pltpu.CompilerParams(vmem_limit_bytes=16 * 1024 * 1024),
    )


def body(embeddings, labels, order):
    rows, width = embeddings.shape
    lanes = lax.axis_size(("x", "z"))
    cap = 2 * rows // lanes
    slot_count = lanes * cap
    wide = width + META
    labels, order = labels.reshape(1, rows), order.reshape(1, rows)

    sent = call(
        lambda *refs: pack_kernel(lanes, *refs),
        jax.ShapeDtypeStruct((slot_count, wide), jnp.bfloat16),
        [VMEM] * 3,
    )(embeddings, labels, order)
    block = lax.all_to_all(sent.reshape(lanes, cap, wide), ("x", "z"), 0, 0, tiled=True)
    block = block.reshape(slot_count, wide)

    other = lax.ppermute(block, "core", [(0, 1), (1, 0)])
    copies = jnp.broadcast_to(block[None], (NY, slot_count, wide))
    lane = lax.all_to_all(copies, "y", 0, 0, tiled=True).reshape(NY * slot_count, wide)
    core = lax.axis_index("core").astype(jnp.int32).reshape(1)
    partial = call(
        gram_kernel,
        jax.ShapeDtypeStruct((2 * lanes, slot_count), jnp.float32),
        [pl.BlockSpec(memory_space=pltpu.SMEM)] + [VMEM] * 3,
    )(core, block, other, lane)
    returned = lax.all_to_all(
        partial.reshape(2 * lanes, 1, slot_count), ("core", "x", "z"), 0, 0, tiled=True
    )
    best = call(pick_kernel, jax.ShapeDtypeStruct((1, rows), jnp.float32), [VMEM] * 2)(
        returned.reshape(2 * lanes, slot_count), labels
    )
    return best.reshape(rows)


def solution(mesh):
    axes = ("y", "core", "x", "z")
    chips = Mesh(mesh.devices.reshape(NY, 2, NX, -1), axes)
    placed = (P(axes, None), P(axes), P(axes))
    return jax.shard_map(body, mesh=chips, in_specs=placed, out_specs=P(axes), check_vma=False)
```

time: 100 us -> 89.4 us (0.89)
  starting transfers between devices: 24.2 us -> 9.75 us
  blocking collectives: 58.5 us -> 67 us
  waiting for transfers between devices: 12.5 us -> 7.1 us
  local copies, waits for them, and re-layouts: 2 us -> 3.55 us
    ppermute x6 -> x1, starting transfers between devices: 24.2 us -> 5.58 us  [body(): other = lax.ppermute(block, 'core', [(0, 1), (1, 0)])]
    ppermute x6 -> x1, waiting for transfers between devices: 12.5 us -> 1.18 us  [body(): other = lax.ppermute(block, 'core', [(0, 1), (1, 0)])]
    all_to_all x3 -> x2, blocking collectives: 58.5 us -> 67 us  [the longest x1 38.9 us: body(): lax.all_to_all(sent.reshape(lanes, cap, wide), ('x', 'z'), 0, 0, tiled=True)]
    all_to_all x0 -> x1, waiting for transfers between devices: none -> 5.92 us  [body(): lax.all_to_all(copies, 'y', 0, 0, tiled=True).reshape(NY * slot_count, wide)]
    all_to_all x0 -> x1, starting transfers between devices: none -> 4.18 us  [body(): lax.all_to_all(copies, 'y', 0, 0, tiled=True).reshape(NY * slot_count, wide)]
    broadcast_in_dim x0 -> x1, local copies, waits for them, and re-layouts: none -> 1.11 us  [body(): copies = jnp.broadcast_to(block[None], (NY, slot_count, wide))]
    unnamed x6 -> x8, local copies, waits for them, and re-layouts: 1.57 us -> 2.22 us
  transfers between devices with their start and end apart: 6 -> 2, of which waited for: 4 -> 2; matrix products, arithmetic and copies ran while one was open for 0% -> 0% of each run, Pallas kernels for 0% -> 0%
where the time goes in v2:
time: 89.4 us; the launch traced here: 89.1 us
  blocking collectives  67 us (75%)
  starting transfers between devices  9.75 us (11%)
  waiting for transfers between devices  7.1 us (8%)
  local copies, waits for them, and re-layouts  3.55 us (4%)
  Pallas kernels  1.68 us (2%)
    all_to_all x1, blocking collectives, body(): lax.all_to_all(sent.reshape(lanes, cap, wide), ('x', 'z'), 0, 0, tiled=True)  38.9 us
    all_to_all x1, blocking collectives, body(): lax.all_to_all(partial.reshape(2 * lanes, 1, slot_count), ('core', 'x', '...  28.1 us
    all_to_all x1, waiting for transfers between devices, body(): lax.all_to_all(copies, 'y', 0, 0, tiled=True).reshape(NY * slot_count, wide)  5.92 us
    ppermute x1, starting transfers between devices, body(): other = lax.ppermute(block, 'core', [(0, 1), (1, 0)])  5.58 us
    all_to_all x1, starting transfers between devices, body(): lax.all_to_all(copies, 'y', 0, 0, tiled=True).reshape(NY * slot_count, wide)  4.18 us
    unnamed x8, local copies, waits for them, and re-layouts  2.22 us
  transfers between devices with their start and end apart: 2, of which 2 were waited for; matrix products, arithmetic and copies ran while one was open for 0% of the time, Pallas kernels for 0%

profile of v2, /device:TPU:1, one launch (start us, length us, event | category | flops | bytes accessed | tf_op | source)
XLA Modules:
  0.0 89.1 jit_solution(14958747143313666108)
XLA Ops:
  0.0 0.0 copy-start
  0.0 0.9 %copy-done = bf16[64,1024]{1,0:T(8,128)(2,1)S(1)} copy-done((bf16[64,1024]{1,0:T(8,128)(2,1)S(1)}, bf16[64,1024]{1,0:T(8,128)(2,1)}, u32[]{:S(2)}) %copy-start) | copy-done | bytes 131096
  0.9 0.0 copy-start.1
  0.9 0.7 copy-done.1
  1.6 0.0 copy-start.3
  1.6 0.7 copy-done.3
  2.2 0.3 shard_map.37
  2.6 0.1 reshape.31
  2.7 38.9 %all_to_all.15 = bf16[64,2,1152]{2,1,0:T(2,128)(2,1)S(1)} all-to-all(bf16[64,2,1152]{2,1,0:T(2,128)(2,1)S(1)} %reshape.31), channel_id=1, replica_groups=mesh['y'=4,'core'=2,'x'=4,'z'=16] {'x','z'}, dimensions={0} | all-to-all | bytes 589824 | tf_op jit(solution)/shard_map/all_to_all | solution.py:118
  41.6 0.1 reshape.32.own_ref
  41.7 1.1 %broadcast_in_dim.2 = bf16[4,128,1152]{2,1,0:T(8,128)(2,1)} broadcast(bf16[128,1152]{1,0:T(8,128)(2,1)S(1)} %reshape.32.own_ref), dimensions={1,2} | broadcast | bytes 1474560 | tf_op jit(solution)/shard_map/broadcast_in_dim | solution.py:122
  42.9 4.2 %all-to-all-start.1 = ((bf16[4,128,1152]{2,1,0:T(8,128)(2,1)}), bf16[4,128,1152]{2,1,0:T(8,128)(2,1)S(1)}, u32[]{:S(2)}, u32[]{:S(2)}) async-start(bf16[4,128,1152]{2,1,0:T(8,128)(2,1)} %broadcast_in_dim.2), calls=%async_computation.1 | async-start | bytes 2359296 | tf_op jit(solution)/shard_map/all_to_all | solution.py:123
  47.0 0.0 copy-start.2
  47.0 5.6 %collective-permute-start = (bf16[128,1152]{1,0:T(8,128)(2,1)S(1)}, bf16[128,1152]{1,0:T(8,128)(2,1)S(1)}, u32[]{:S(2)}, u32[]{:S(2)}) collective-permute-start(bf16[128,1152]{1,0:T(8,128)(2,1)S(1)} %reshape.32.own_ref), channel_id=1, source_target_pairs={{0,64},{64,0},{1,65},{65,1},{2,66},{66,2},{3,67},{67,3},{4,68},{68... | collective-permute-start | bytes 884744 | tf_op jit(solution)/shard_map/ppermute | solution.py:121
  52.6 1.2 %collective-permute-done.other_ref = bf16[128,1152]{1,0:T(8,128)(2,1)S(1)} collective-permute-done((bf16[128,1152]{1,0:T(8,128)(2,1)S(1)}, bf16[128,1152]{1,0:T(8,128)(2,1)S(1)}, u32[]{:S(2)}, u32[]{:S(2)}) %collective-permute-start) | collective-permute-done | bytes 294944 | tf_op jit(solution)/shard_map/ppermute | solution.py:121
  53.8 5.9 %all-to-all-done.1 = bf16[4,128,1152]{2,1,0:T(8,128)(2,1)S(1)} async-done(((bf16[4,128,1152]{2,1,0:T(8,128)(2,1)}), bf16[4,128,1152]{2,1,0:T(8,128)(2,1)S(1)}, u32[]{:S(2)}, u32[]{:S(2)}) %all-to-all-start.1) | async-done | bytes 1179680 | tf_op jit(solution)/shard_map/all_to_all | solution.py:123
  59.7 0.7 shard_map.38
  60.4 28.1 %all_to_all.16 = f32[128,1,128]{2,1,0:T(1,128)S(1)} all-to-all(f32[128,1,128]{2,1,0:T(1,128)S(1)} %bitcast.10), channel_id=1, replica_groups=mesh['y'=4,'core'=2,'x'=4,'z'=16] {'core','x','z'}, dimensions={0} | all-to-all | bytes 131072 | tf_op jit(solution)/shard_map/all_to_all | solution.py:130
  88.5 0.0 copy-done.2
  88.5 0.7 shard_map.39
Async XLA Ops:
  0.0 0.9 %copy-start = (bf16[64,1024]{1,0:T(8,128)(2,1)S(1)}, bf16[64,1024]{1,0:T(8,128)(2,1)}, u32[]{:S(2)}) copy-start(bf16[64,1024]{1,0:T(8,128)(2,1)} %refs_0_.1) | copy-start | bytes 393220
  0.9 0.7 copy-start.1
  1.6 0.7 copy-start.3
  42.9 16.9 %all-to-all-start.1 = ((bf16[4,128,1152]{2,1,0:T(8,128)(2,1)}), bf16[4,128,1152]{2,1,0:T(8,128)(2,1)S(1)}, u32[]{:S(2)}, u32[]{:S(2)}) async-start(bf16[4,128,1152]{2,1,0:T(8,128)(2,1)} %broadcast_in_dim.2), calls=%async_computation.1 | async-start | bytes 2359296 | tf_op jit(solution)/shard_map/all_to_all | solution.py:123
  47.0 41.4 %copy-start.2 = (s32[64]{0:T(128)S(1)}, s32[64]{0:T(128)}, u32[]{:S(2)}) copy-start(s32[64]{0:T(128)} %param.4) | copy-start | bytes 772
  47.0 6.8 %collective-permute-start = (bf16[128,1152]{1,0:T(8,128)(2,1)S(1)}, bf16[128,1152]{1,0:T(8,128)(2,1)S(1)}, u32[]{:S(2)}, u32[]{:S(2)}) collective-permute-start(bf16[128,1152]{1,0:T(8,128)(2,1)S(1)} %reshape.32.own_ref), channel_id=1, source_target_pairs={{0,64},{64,0},{1,65},{65,1},{2,66},{66,2},{3,67},{67,3},{4,68},{68... | collective-permute-start | bytes 884744 | tf_op jit(solution)/shard_map/ppermute | solution.py:121

commit v3 on v2

--- a/solution.py
+++ b/solution.py
@@ -26,7 +26,17 @@
     return target, hit, place
 
 
-def pack_kernel(lanes, emb_ref, labels_ref, order_ref, out_ref):
+def pack_kernel(lanes, emb_hbm, labels_hbm, order_hbm, out_ref, emb_ref, labels_ref, order_ref, arrived):
+    copies = [
+        pltpu.make_async_copy(source, target, arrived.at[k])
+        for k, (source, target) in enumerate(
+            [(emb_hbm, emb_ref), (labels_hbm, labels_ref), (order_hbm, order_ref)]
+        )
+    ]
+    for copy in copies:
+        copy.start()
+    for copy in copies:
+        copy.wait()
     rows, width = emb_ref.shape
     slot_count = out_ref.shape[0]
     floats = emb_ref[...].astype(jnp.float32)
@@ -51,11 +61,14 @@
     out_ref[:, width:] = meta.astype(jnp.bfloat16)
 
 
-def gram_kernel(core_ref, own_ref, other_ref, lane_ref, out_ref):
+def copies_kernel(block_ref, out_ref):
+    for k in range(out_ref.shape[0]):
+        out_ref[k] = block_ref[...]
+
+
+def gram_kernel(own_ref, other_ref, lane_ref, own_out, other_out):
     width = own_ref.shape[1] - META
     size = own_ref.shape[0]
-    dests = out_ref.shape[0] // 2
-    core = core_ref[0]
     queries = jnp.concatenate([own_ref[...], other_ref[...]], axis=0)
     members = lane_ref[...]
     scores = lax.dot_general(
@@ -71,20 +84,24 @@
     order_down = down[:, 1:2] * 256.0 + down[:, 2:3]
     valid = (label_down == across[0:1, :]) & (order_down < across[1:2, :])
     best = jnp.max(jnp.where(valid, scores, -1.0), axis=0, keepdims=True)
-    own, other = best[:, :size], best[:, size:]
+    own_out[...] = best[:, :size]
+    other_out[...] = best[:, size:]
+
+
+def spread_kernel(own_ref, back_ref, out_ref):
+    dests, size = out_ref.shape
+    best = jnp.maximum(own_ref[...], back_ref[...])
     home = lax.broadcasted_iota(jnp.int32, (dests, size), 0)
     slot = lax.broadcasted_iota(jnp.int32, (dests, size), 1) // (size // dests)
-    mine = home == slot
-    out_ref[:dests, :] = jnp.where(mine, jnp.where(core == 0, own, other), -4.0)
-    out_ref[dests:, :] = jnp.where(mine, jnp.where(core == 0, other, own), -4.0)
+    out_ref[...] = jnp.where(home == slot, best, -4.0)
 
 
 def pick_kernel(returned_ref, labels_ref, out_ref):
-    lanes, size = returned_ref.shape[0] // 2, returned_ref.shape[1]
+    lanes, size = returned_ref.shape
     _, hit, place = slots(labels_ref[...], lanes)
     cap = size // lanes
     lane = lax.rem(lax.broadcasted_iota(jnp.int32, (lanes, size), 1), cap)
-    returned = jnp.maximum(returned_ref[:lanes, :], returned_ref[lanes:, :])
+    returned = returned_ref[...]
     best = jnp.full(hit.shape, -4.0, jnp.float32)
     for p in range(cap):
         value = jnp.max(jnp.where(lane == p, returned, -4.0), axis=1, keepdims=True)
@@ -92,12 +109,13 @@
     out_ref[...] = jnp.max(best, axis=0, keepdims=True)
 
 
-def call(kernel, outs, specs):
+def call(kernel, outs, specs, scratch=()):
     return pl.pallas_call(
         kernel,
         out_shape=outs,
         in_specs=specs,
         out_specs=jax.tree.map(lambda _: VMEM, outs),
+        scratch_shapes=scratch,
         compiler_params=pltpu.CompilerParams(vmem_limit_bytes=16 * 1024 * 1024),
     )
 
@@ -113,25 +131,32 @@
     sent = call(
         lambda *refs: pack_kernel(lanes, *refs),
         jax.ShapeDtypeStruct((slot_count, wide), jnp.bfloat16),
-        [VMEM] * 3,
+        [pl.BlockSpec(memory_space=pltpu.HBM)] * 3,
+        [
+            pltpu.VMEM((rows, width), jnp.bfloat16),
+            pltpu.VMEM((1, rows), jnp.int32),
+            pltpu.VMEM((1, rows), jnp.int32),
+            pltpu.SemaphoreType.DMA((3,)),
+        ],
     )(embeddings, labels, order)
     block = lax.all_to_all(sent.reshape(lanes, cap, wide), ("x", "z"), 0, 0, tiled=True)
     block = block.reshape(slot_count, wide)
 
-    other = lax.ppermute(block, "core", [(0, 1), (1, 0)])
-    copies = jnp.broadcast_to(block[None], (NY, slot_count, wide))
+    swap = [(0, 1), (1, 0)]
+    other = lax.ppermute(block, "core", swap)
+    copies = call(
+        copies_kernel, jax.ShapeDtypeStruct((NY, slot_count, wide), jnp.bfloat16), [VMEM]
+    )(block)
     lane = lax.all_to_all(copies, "y", 0, 0, tiled=True).reshape(NY * slot_count, wide)
-    core = lax.axis_index("core").astype(jnp.int32).reshape(1)
-    partial = call(
-        gram_kernel,
-        jax.ShapeDtypeStruct((2 * lanes, slot_count), jnp.float32),
-        [pl.BlockSpec(memory_space=pltpu.SMEM)] + [VMEM] * 3,
-    )(core, block, other, lane)
-    returned = lax.all_to_all(
-        partial.reshape(2 * lanes, 1, slot_count), ("core", "x", "z"), 0, 0, tiled=True
-    )
+    own_best, other_best = call(
+        gram_kernel, [jax.ShapeDtypeStruct((1, slot_count), jnp.float32)] * 2, [VMEM] * 3
+    )(block, other, lane)
+    spread = call(
+        spread_kernel, jax.ShapeDtypeStruct((lanes, slot_count), jnp.float32), [VMEM] * 2
+    )(own_best, lax.ppermute(other_best, "core", swap))
+    returned = lax.all_to_all(spread.reshape(lanes, 1, slot_count), ("x", "z"), 0, 0, tiled=True)
     best = call(pick_kernel, jax.ShapeDtypeStruct((1, rows), jnp.float32), [VMEM] * 2)(
-        returned.reshape(2 * lanes, slot_count), labels
+        returned.reshape(lanes, slot_count), labels
     )
     return best.reshape(rows)
 

time: 89.4 us -> 90.3 us (1.010)
  blocking collectives: 67 us -> 60.1 us
  starting transfers between devices: 9.75 us -> 16.5 us
  Pallas kernels: 1.68 us -> 2.97 us
  local copies, waits for them, and re-layouts: 3.55 us -> 2.44 us
    all_to_all x1, blocking collectives: 28.1 us -> 21.2 us  [body(): lax.all_to_all(spread.reshape(lanes, 1, slot_count), ('x', 'z'), 0, 0, ti...]
    ppermute x1 -> x2, starting transfers between devices: 5.58 us -> 12.3 us  [the longest x1 6.7 us: body(): lax.ppermute(other_best, 'core', swap)]
    pallas_call x1 -> x3, Pallas kernels: 0.67 us -> 1.78 us  [the longest x1 1.12 us: body(): call(copies_kernel, jax.ShapeDtypeStruct((NY, slot_count, wide), jnp.bflo...]
    broadcast_in_dim x1 -> x0, local copies, waits for them, and re-layouts: 1.11 us -> none  [body(): copies = jnp.broadcast_to(block[None], (NY, slot_count, wide))]
    ppermute x1 -> x2, waiting for transfers between devices: 1.18 us -> 1.98 us  [the longest x1 1.19 us: body(): other = lax.ppermute(block, 'core', swap)]
  transfers between devices with their start and end apart: 2 -> 3, of which waited for: 2 -> 3; matrix products, arithmetic and copies ran while one was open for 0% -> 0% of each run, Pallas kernels for 0% -> 0%
where the time goes in v3:
time: 90.3 us; the launch traced here: 89.9 us
  blocking collectives  60.1 us (67%)
  starting transfers between devices  16.5 us (18%)
  waiting for transfers between devices  7.9 us (9%)
  Pallas kernels  2.97 us (3%)
  local copies, waits for them, and re-layouts  2.44 us (3%)
    all_to_all x1, blocking collectives, body(): lax.all_to_all(sent.reshape(lanes, cap, wide), ('x', 'z'), 0, 0, tiled=True)  38.9 us
    all_to_all x1, blocking collectives, body(): lax.all_to_all(spread.reshape(lanes, 1, slot_count), ('x', 'z'), 0, 0, ti...  21.2 us
    ppermute x1, starting transfers between devices, body(): lax.ppermute(other_best, 'core', swap)  6.7 us
    all_to_all x1, waiting for transfers between devices, body(): lax.all_to_all(copies, 'y', 0, 0, tiled=True).reshape(NY * slot_count, wide)  5.92 us
    ppermute x1, starting transfers between devices, body(): other = lax.ppermute(block, 'core', swap)  5.58 us
    all_to_all x1, starting transfers between devices, body(): lax.all_to_all(copies, 'y', 0, 0, tiled=True).reshape(NY * slot_count, wide)  4.18 us
    unnamed x8, local copies, waits for them, and re-layouts  2.22 us
  transfers between devices with their start and end apart: 3, of which 3 were waited for; matrix products, arithmetic and copies ran while one was open for 0% of the time, Pallas kernels for 0%

profile of v3, /device:TPU:1, one launch (start us, length us, event | category | flops | bytes accessed | tf_op | source)
XLA Modules:
  0.0 89.9 jit_solution(3732399446923150984)
XLA Ops:
  0.0 0.0 copy-start
  0.0 0.9 %copy-done = bf16[64,1024]{1,0:T(8,128)(2,1)S(1)} copy-done((bf16[64,1024]{1,0:T(8,128)(2,1)S(1)}, bf16[64,1024]{1,0:T(8,128)(2,1)}, u32[]{:S(2)}) %copy-start) | copy-done | bytes 131096
  0.9 0.0 copy-start.1
  0.9 0.7 copy-done.1
  1.6 0.0 copy-start.3
  1.6 0.7 copy-done.3
  2.2 0.5 shard_map.37
  2.7 0.1 reshape.26
  2.9 38.9 %all_to_all.15 = bf16[64,2,1152]{2,1,0:T(2,128)(2,1)S(1)} all-to-all(bf16[64,2,1152]{2,1,0:T(2,128)(2,1)S(1)} %reshape.26), channel_id=1, replica_groups=mesh['y'=4,'core'=2,'x'=4,'z'=16] {'x','z'}, dimensions={0} | all-to-all | bytes 589824 | tf_op jit(solution)/shard_map/all_to_all | solution.py:142
  41.8 0.1 reshape.27.block_ref.own_ref
  41.9 1.1 %shard_map.38 = bf16[4,128,1152]{2,1,0:T(8,128)(2,1)} custom-call(bf16[128,1152]{1,0:T(8,128)(2,1)S(1)} %reshape.27.block_ref.own_ref), custom_call_target="tpu_custom_call" | custom-call | tf_op jit(solution)/shard_map/pallas_call | solution.py:147
  43.0 4.2 %all-to-all-start.1 = ((bf16[4,128,1152]{2,1,0:T(8,128)(2,1)}), bf16[4,128,1152]{2,1,0:T(8,128)(2,1)S(1)}, u32[]{:S(2)}, u32[]{:S(2)}) async-start(bf16[4,128,1152]{2,1,0:T(8,128)(2,1)} %shard_map.38), calls=%async_computation.1 | async-start | bytes 2359296 | tf_op jit(solution)/shard_map/all_to_all | solution.py:150
  47.2 0.0 copy-start.2
  47.2 5.6 %collective-permute-start = (bf16[128,1152]{1,0:T(8,128)(2,1)S(1)}, bf16[128,1152]{1,0:T(8,128)(2,1)S(1)}, u32[]{:S(2)}, u32[]{:S(2)}) collective-permute-start(bf16[128,1152]{1,0:T(8,128)(2,1)S(1)} %reshape.27.block_ref.own_ref), channel_id=1, source_target_pairs={{0,64},{64,0},{1,65},{65,1},{2,66},{66,2},{3,67},{67,3},{4,68},{68... | collective-permute-start | bytes 884744 | tf_op jit(solution)/shard_map/ppermute | solution.py:146
  52.8 1.2 %collective-permute-done.other_ref = bf16[128,1152]{1,0:T(8,128)(2,1)S(1)} collective-permute-done((bf16[128,1152]{1,0:T(8,128)(2,1)S(1)}, bf16[128,1152]{1,0:T(8,128)(2,1)S(1)}, u32[]{:S(2)}, u32[]{:S(2)}) %collective-permute-start) | collective-permute-done | bytes 294944 | tf_op jit(solution)/shard_map/ppermute | solution.py:146
  54.0 5.9 %all-to-all-done.1 = bf16[4,128,1152]{2,1,0:T(8,128)(2,1)S(1)} async-done(((bf16[4,128,1152]{2,1,0:T(8,128)(2,1)}), bf16[4,128,1152]{2,1,0:T(8,128)(2,1)S(1)}, u32[]{:S(2)}, u32[]{:S(2)}) %all-to-all-start.1) | async-done | bytes 1179680 | tf_op jit(solution)/shard_map/all_to_all | solution.py:150
  59.9 0.7 shard_map.39
  60.6 6.7 %collective-permute-start.1 = (f32[1,128]{1,0:T(1,128)S(1)}, f32[1,128]{1,0:T(1,128)S(1)}, u32[]{:S(2)}, u32[]{:S(2)}) collective-permute-start(f32[1,128]{1,0:T(1,128)S(1)} %get-tuple-element.8), channel_id=1, source_target_pairs={{0,64},{64,0},{1,65},{65,1},{2,66},{66,2},{3,67},{67,3},{4,68},{68... | collective-permute-start | bytes 1544 | tf_op jit(solution)/shard_map/ppermute | solution.py:156
  67.3 0.8 collective-permute-done.1.back_ref
  68.1 21.2 %all_to_all.16 = f32[64,1,128]{2,1,0:T(1,128)S(1)} all-to-all(f32[64,1,128]{2,1,0:T(1,128)S(1)} %bitcast.9), channel_id=1, replica_groups=mesh['y'=4,'core'=2,'x'=4,'z'=16] {'x','z'}, dimensions={0} | all-to-all | bytes 65536 | tf_op jit(solution)/shard_map/all_to_all | solution.py:157
  89.3 0.0 copy-done.2
  89.3 0.7 shard_map.41
  (1 shorter events, 0.0 us)
Async XLA Ops:
  0.0 0.9 %copy-start = (bf16[64,1024]{1,0:T(8,128)(2,1)S(1)}, bf16[64,1024]{1,0:T(8,128)(2,1)}, u32[]{:S(2)}) copy-start(bf16[64,1024]{1,0:T(8,128)(2,1)} %refs_0_.1) | copy-start | bytes 393220
  0.9 0.7 copy-start.1
  1.6 0.7 copy-start.3
  43.0 16.9 %all-to-all-start.1 = ((bf16[4,128,1152]{2,1,0:T(8,128)(2,1)}), bf16[4,128,1152]{2,1,0:T(8,128)(2,1)S(1)}, u32[]{:S(2)}, u32[]{:S(2)}) async-start(bf16[4,128,1152]{2,1,0:T(8,128)(2,1)} %shard_map.38), calls=%async_computation.1 | async-start | bytes 2359296 | tf_op jit(solution)/shard_map/all_to_all | solution.py:150
  47.2 42.0 %copy-start.2 = (s32[64]{0:T(128)S(1)}, s32[64]{0:T(128)}, u32[]{:S(2)}) copy-start(s32[64]{0:T(128)} %param.4) | copy-start | bytes 772
  47.2 6.8 %collective-permute-start = (bf16[128,1152]{1,0:T(8,128)(2,1)S(1)}, bf16[128,1152]{1,0:T(8,128)(2,1)S(1)}, u32[]{:S(2)}, u32[]{:S(2)}) collective-permute-start(bf16[128,1152]{1,0:T(8,128)(2,1)S(1)} %reshape.27.block_ref.own_ref), channel_id=1, source_target_pairs={{0,64},{64,0},{1,65},{65,1},{2,66},{66,2},{3,67},{67,3},{4,68},{68... | collective-permute-start | bytes 884744 | tf_op jit(solution)/shard_map/ppermute | solution.py:146
  60.6 7.5 %collective-permute-start.1 = (f32[1,128]{1,0:T(1,128)S(1)}, f32[1,128]{1,0:T(1,128)S(1)}, u32[]{:S(2)}, u32[]{:S(2)}) collective-permute-start(f32[1,128]{1,0:T(1,128)S(1)} %get-tuple-element.8), channel_id=1, source_target_pairs={{0,64},{64,0},{1,65},{65,1},{2,66},{66,2},{3,67},{67,3},{4,68},{68... | collective-permute-start | bytes 1544 | tf_op jit(solution)/shard_map/ppermute | solution.py:156

commit v4 on v2

--- a/solution.py
+++ b/solution.py
@@ -26,29 +26,38 @@
     return target, hit, place
 
 
-def pack_kernel(lanes, emb_ref, labels_ref, order_ref, out_ref):
+def pack_kernel(lanes, emb_hbm, labels_hbm, order_hbm, out_ref, emb_ref, labels_ref, order_ref, arrived):
+    parts = [(labels_hbm, labels_ref), (order_hbm, order_ref), (emb_hbm, emb_ref)]
+    copies = [
+        pltpu.make_async_copy(source, target, arrived.at[k]) for k, (source, target) in enumerate(parts)
+    ]
+    for copy in copies:
+        copy.start()
     rows, width = emb_ref.shape
     slot_count = out_ref.shape[0]
-    floats = emb_ref[...].astype(jnp.float32)
-    scale = lax.rsqrt(jnp.sum(floats * floats, axis=1, keepdims=True) + width * EPSILON)
-    unit = (floats * scale).astype(jnp.bfloat16)
-    labels = labels_ref[...]
+    copies[0].wait()
+    copies[1].wait()
+    labels, order = labels_ref[...], order_ref[...]
     target, _, place = slots(labels, lanes)
     cap = slot_count // lanes
     here = lax.broadcasted_iota(jnp.int32, (slot_count, rows), 0) == target * cap + place
-    out_ref[:, :width] = jnp.dot(
-        here.astype(jnp.bfloat16), unit, preferred_element_type=jnp.float32
-    ).astype(jnp.bfloat16)
 
     def column(values):
         return jnp.sum(jnp.where(here, values.astype(jnp.float32), 0.0), axis=1, keepdims=True)
 
-    order = order_ref[...]
     lane = lax.broadcasted_iota(jnp.int32, (slot_count, META), 1)
     meta = jnp.where(lane == 0, column(labels // lanes + 1), 0.0)
     meta = jnp.where(lane == 1, column(order // 256), meta)
     meta = jnp.where(lane == 2, column(lax.rem(order, 256)), meta)
     out_ref[:, width:] = meta.astype(jnp.bfloat16)
+
+    copies[2].wait()
+    floats = emb_ref[...].astype(jnp.float32)
+    scale = lax.rsqrt(jnp.sum(floats * floats, axis=1, keepdims=True) + width * EPSILON)
+    unit = (floats * scale).astype(jnp.bfloat16)
+    out_ref[:, :width] = jnp.dot(
+        here.astype(jnp.bfloat16), unit, preferred_element_type=jnp.float32
+    ).astype(jnp.bfloat16)
 
 
 def gram_kernel(core_ref, own_ref, other_ref, lane_ref, out_ref):
@@ -92,12 +101,13 @@
     out_ref[...] = jnp.max(best, axis=0, keepdims=True)
 
 
-def call(kernel, outs, specs):
+def call(kernel, outs, specs, scratch=()):
     return pl.pallas_call(
         kernel,
         out_shape=outs,
         in_specs=specs,
         out_specs=jax.tree.map(lambda _: VMEM, outs),
+        scratch_shapes=scratch,
         compiler_params=pltpu.CompilerParams(vmem_limit_bytes=16 * 1024 * 1024),
     )
 
@@ -113,8 +123,14 @@
     sent = call(
         lambda *refs: pack_kernel(lanes, *refs),
         jax.ShapeDtypeStruct((slot_count, wide), jnp.bfloat16),
-        [VMEM] * 3,
-    )(embeddings, labels, order)
+        [pl.BlockSpec(memory_space=pltpu.HBM)] * 3,
+        [
+            pltpu.VMEM((rows, width), jnp.bfloat16),
+            pltpu.VMEM((1, rows), jnp.int32),
+            pltpu.VMEM((1, rows), jnp.int32),
+            pltpu.SemaphoreType.DMA((3,)),
+        ],
+    )(*[pltpu.with_memory_space_constraint(a, pltpu.HBM) for a in (embeddings, labels, order)])
     block = lax.all_to_all(sent.reshape(lanes, cap, wide), ("x", "z"), 0, 0, tiled=True)
     block = block.reshape(slot_count, wide)
 

time: 89.4 us -> 88.1 us (0.985)
  local copies, waits for them, and re-layouts: 3.55 us -> 1.33 us
  Pallas kernels: 1.68 us -> 2.62 us
    unnamed x8 -> x2, local copies, waits for them, and re-layouts: 2.22 us -> 0.01 us
    pallas_call x1, Pallas kernels: 0.35 us -> 1.28 us  [body(): call(lambda *refs: pack_kernel(lanes, *refs), jax.ShapeDtypeStruct((slot_...]
where the time goes in v4:
time: 88.1 us; the launch traced here: 87.9 us
  blocking collectives  67 us (76%)
  starting transfers between devices  9.76 us (11%)
  waiting for transfers between devices  7.1 us (8%)
  Pallas kernels  2.62 us (3%)
  local copies, waits for them, and re-layouts  1.33 us (2%)
    all_to_all x1, blocking collectives, body(): lax.all_to_all(sent.reshape(lanes, cap, wide), ('x', 'z'), 0, 0, tiled=True)  38.9 us
    all_to_all x1, blocking collectives, body(): lax.all_to_all(partial.reshape(2 * lanes, 1, slot_count), ('core', 'x', '...  28.1 us
    all_to_all x1, waiting for transfers between devices, body(): lax.all_to_all(copies, 'y', 0, 0, tiled=True).reshape(NY * slot_count, wide)  5.92 us
    ppermute x1, starting transfers between devices, body(): other = lax.ppermute(block, 'core', [(0, 1), (1, 0)])  5.58 us
    all_to_all x1, starting transfers between devices, body(): lax.all_to_all(copies, 'y', 0, 0, tiled=True).reshape(NY * slot_count, wide)  4.19 us
  transfers between devices with their start and end apart: 2, of which 2 were waited for; matrix products, arithmetic and copies ran while one was open for 0% of the time, Pallas kernels for 0%

profile of v4, /device:TPU:1, one launch (start us, length us, event | category | flops | bytes accessed | tf_op | source)
XLA Modules:
  0.0 87.9 jit_solution(6496105271886063947)
XLA Ops:
  0.0 1.3 %shard_map.37 = bf16[128,1152]{1,0:T(8,128)(2,1)S(1)} custom-call(bf16[64,1024]{1,0:T(8,128)(2,1)} %refs_0_.1, s32[1,64]{1,0:T(1,128)} %bitcast.12, s32[1,64]{1,0:T(1,128)} %bitcast.14), custom_call_target="tpu_custom_call" | custom-call | tf_op jit(solution)/shard_map/pallas_call | solution.py:123
  1.3 0.1 reshape.31
  1.4 38.9 %all_to_all.15 = bf16[64,2,1152]{2,1,0:T(2,128)(2,1)S(1)} all-to-all(bf16[64,2,1152]{2,1,0:T(2,128)(2,1)S(1)} %reshape.31), channel_id=1, replica_groups=mesh['y'=4,'core'=2,'x'=4,'z'=16] {'x','z'}, dimensions={0} | all-to-all | bytes 589824 | tf_op jit(solution)/shard_map/all_to_all | solution.py:134
  40.4 0.1 reshape.32.own_ref
  40.5 1.1 %broadcast_in_dim.2 = bf16[4,128,1152]{2,1,0:T(8,128)(2,1)} broadcast(bf16[128,1152]{1,0:T(8,128)(2,1)S(1)} %reshape.32.own_ref), dimensions={1,2} | broadcast | bytes 1474560 | tf_op jit(solution)/shard_map/broadcast_in_dim | solution.py:138
  41.6 4.2 %all-to-all-start.1 = ((bf16[4,128,1152]{2,1,0:T(8,128)(2,1)}), bf16[4,128,1152]{2,1,0:T(8,128)(2,1)S(1)}, u32[]{:S(2)}, u32[]{:S(2)}) async-start(bf16[4,128,1152]{2,1,0:T(8,128)(2,1)} %broadcast_in_dim.2), calls=%async_computation.1 | async-start | bytes 2359296 | tf_op jit(solution)/shard_map/all_to_all | solution.py:139
  45.8 0.0 copy-start
  45.8 5.6 %collective-permute-start = (bf16[128,1152]{1,0:T(8,128)(2,1)S(1)}, bf16[128,1152]{1,0:T(8,128)(2,1)S(1)}, u32[]{:S(2)}, u32[]{:S(2)}) collective-permute-start(bf16[128,1152]{1,0:T(8,128)(2,1)S(1)} %reshape.32.own_ref), channel_id=1, source_target_pairs={{0,64},{64,0},{1,65},{65,1},{2,66},{66,2},{3,67},{67,3},{4,68},{68... | collective-permute-start | bytes 884744 | tf_op jit(solution)/shard_map/ppermute | solution.py:137
  51.3 1.2 %collective-permute-done.other_ref = bf16[128,1152]{1,0:T(8,128)(2,1)S(1)} collective-permute-done((bf16[128,1152]{1,0:T(8,128)(2,1)S(1)}, bf16[128,1152]{1,0:T(8,128)(2,1)S(1)}, u32[]{:S(2)}, u32[]{:S(2)}) %collective-permute-start) | collective-permute-done | bytes 294944 | tf_op jit(solution)/shard_map/ppermute | solution.py:137
  52.5 5.9 %all-to-all-done.1 = bf16[4,128,1152]{2,1,0:T(8,128)(2,1)S(1)} async-done(((bf16[4,128,1152]{2,1,0:T(8,128)(2,1)}), bf16[4,128,1152]{2,1,0:T(8,128)(2,1)S(1)}, u32[]{:S(2)}, u32[]{:S(2)}) %all-to-all-start.1) | async-done | bytes 1179680 | tf_op jit(solution)/shard_map/all_to_all | solution.py:139
  58.4 0.7 shard_map.38
  59.1 28.1 %all_to_all.16 = f32[128,1,128]{2,1,0:T(1,128)S(1)} all-to-all(f32[128,1,128]{2,1,0:T(1,128)S(1)} %bitcast.10), channel_id=1, replica_groups=mesh['y'=4,'core'=2,'x'=4,'z'=16] {'core','x','z'}, dimensions={0} | all-to-all | bytes 131072 | tf_op jit(solution)/shard_map/all_to_all | solution.py:146
  87.2 0.0 copy-done
  87.2 0.7 shard_map.39
Async XLA Ops:
  41.6 16.9 %all-to-all-start.1 = ((bf16[4,128,1152]{2,1,0:T(8,128)(2,1)}), bf16[4,128,1152]{2,1,0:T(8,128)(2,1)S(1)}, u32[]{:S(2)}, u32[]{:S(2)}) async-start(bf16[4,128,1152]{2,1,0:T(8,128)(2,1)} %broadcast_in_dim.2), calls=%async_computation.1 | async-start | bytes 2359296 | tf_op jit(solution)/shard_map/all_to_all | solution.py:139
  45.8 41.4 %copy-start = (s32[64]{0:T(128)S(1)}, s32[64]{0:T(128)}, u32[]{:S(2)}) copy-start(s32[64]{0:T(128)} %param.4) | copy-start | bytes 772
  45.8 6.8 %collective-permute-start = (bf16[128,1152]{1,0:T(8,128)(2,1)S(1)}, bf16[128,1152]{1,0:T(8,128)(2,1)S(1)}, u32[]{:S(2)}, u32[]{:S(2)}) collective-permute-start(bf16[128,1152]{1,0:T(8,128)(2,1)S(1)} %reshape.32.own_ref), channel_id=1, source_target_pairs={{0,64},{64,0},{1,65},{65,1},{2,66},{66,2},{3,67},{67,3},{4,68},{68... | collective-permute-start | bytes 884744 | tf_op jit(solution)/shard_map/ppermute | solution.py:137

commit v5 on v4

--- a/solution.py
+++ b/solution.py
@@ -7,6 +7,8 @@
 from jax.sharding import PartitionSpec as P
 
 EPSILON = 1e-06
+DOWN, ACROSS = 4, 4
+SERIAL = 7
 NX = 4
 NY = 4
 META = 128
@@ -26,14 +28,29 @@
     return target, hit, place
 
 
-def pack_kernel(lanes, emb_hbm, labels_hbm, order_hbm, out_ref, emb_ref, labels_ref, order_ref, arrived):
-    parts = [(labels_hbm, labels_ref), (order_hbm, order_ref), (emb_hbm, emb_ref)]
+def pack_kernel(lanes, core_ref, emb_hbm, labels_hbm, order_hbm, out_ref, emb_ref, labels_ref, order_ref, arrived):
+    rows, width = emb_ref.shape
+    tall, wide = rows // DOWN, width // ACROSS
+    pieces = [(pl.ds(r * tall, tall), pl.ds(c * wide, wide)) for r in range(DOWN) for c in range(ACROSS)]
+    parts = [(labels_hbm, labels_ref), (order_hbm, order_ref)]
+    parts += [(emb_hbm.at[piece], emb_ref.at[piece]) for piece in pieces]
     copies = [
         pltpu.make_async_copy(source, target, arrived.at[k]) for k, (source, target) in enumerate(parts)
     ]
-    for copy in copies:
+    paced, others = copies[2 : 2 + SERIAL], copies[2 + SERIAL :]
+    goes_first = core_ref[0] == 1
+    for copy in copies[:2]:
         copy.start()
-    rows, width = emb_ref.shape
+    for copy in paced:
+        copy.start()
+
+        @pl.when(jnp.logical_not(goes_first))
+        def _():
+            copy.wait()
+
+    for copy in others:
+        copy.start()
+
     slot_count = out_ref.shape[0]
     copies[0].wait()
     copies[1].wait()
@@ -51,7 +68,14 @@
     meta = jnp.where(lane == 2, column(lax.rem(order, 256)), meta)
     out_ref[:, width:] = meta.astype(jnp.bfloat16)
 
-    copies[2].wait()
+    for copy in others:
+        copy.wait()
+
+    @pl.when(goes_first)
+    def _():
+        for copy in paced:
+            copy.wait()
+
     floats = emb_ref[...].astype(jnp.float32)
     scale = lax.rsqrt(jnp.sum(floats * floats, axis=1, keepdims=True) + width * EPSILON)
     unit = (floats * scale).astype(jnp.bfloat16)
@@ -120,24 +144,24 @@
     wide = width + META
     labels, order = labels.reshape(1, rows), order.reshape(1, rows)
 
+    core = lax.axis_index("core").astype(jnp.int32).reshape(1)
     sent = call(
         lambda *refs: pack_kernel(lanes, *refs),
         jax.ShapeDtypeStruct((slot_count, wide), jnp.bfloat16),
-        [pl.BlockSpec(memory_space=pltpu.HBM)] * 3,
+        [pl.BlockSpec(memory_space=pltpu.SMEM)] + [pl.BlockSpec(memory_space=pltpu.HBM)] * 3,
         [
             pltpu.VMEM((rows, width), jnp.bfloat16),
             pltpu.VMEM((1, rows), jnp.int32),
             pltpu.VMEM((1, rows), jnp.int32),
-            pltpu.SemaphoreType.DMA((3,)),
+            pltpu.SemaphoreType.DMA((2 + DOWN * ACROSS,)),
         ],
-    )(*[pltpu.with_memory_space_constraint(a, pltpu.HBM) for a in (embeddings, labels, order)])
+    )(core, *[pltpu.with_memory_space_constraint(a, pltpu.HBM) for a in (embeddings, labels, order)])
     block = lax.all_to_all(sent.reshape(lanes, cap, wide), ("x", "z"), 0, 0, tiled=True)
     block = block.reshape(slot_count, wide)
 
     other = lax.ppermute(block, "core", [(0, 1), (1, 0)])
     copies = jnp.broadcast_to(block[None], (NY, slot_count, wide))
     lane = lax.all_to_all(copies, "y", 0, 0, tiled=True).reshape(NY * slot_count, wide)
-    core = lax.axis_index("core").astype(jnp.int32).reshape(1)
     partial = call(
         gram_kernel,
         jax.ShapeDtypeStruct((2 * lanes, slot_count), jnp.float32),

time: 88.1 us -> 84.5 us (0.959)
  waiting for transfers between devices: 7.1 us -> 1.19 us
  starting transfers between devices: 9.76 us -> 13.5 us
  blocking collectives: 67 us -> 65.1 us
    all_to_all x1, waiting for transfers between devices: 5.92 us -> 0.01 us  [body(): lax.all_to_all(copies, 'y', 0, 0, tiled=True).reshape(NY * slot_count, wide)]
    all_to_all x1, blocking collectives: 38.9 us -> 35.1 us  [body(): lax.all_to_all(sent.reshape(lanes, cap, wide), ('x', 'z'), 0, 0, tiled=True)]
    ppermute x1, starting transfers between devices: 5.58 us -> 9.27 us  [body(): other = lax.ppermute(block, 'core', [(0, 1), (1, 0)])]
    all_to_all x1, blocking collectives: 28.1 us -> 30 us  [body(): lax.all_to_all(partial.reshape(2 * lanes, 1, slot_count), ('core', 'x', '...]
  transfers between devices with their start and end apart: 2 -> 2, of which waited for: 2 -> 1; matrix products, arithmetic and copies ran while one was open for 0% -> 0% of each run, Pallas kernels for 0% -> 0%
where the time goes in v5:
time: 84.5 us; the launch traced here: 83.9 us
  blocking collectives  65.1 us (77%)
  starting transfers between devices  13.5 us (16%)
  Pallas kernels  2.79 us (3%)
  local copies, waits for them, and re-layouts  1.33 us (2%)
  waiting for transfers between devices  1.19 us (1%)
    all_to_all x1, blocking collectives, body(): lax.all_to_all(sent.reshape(lanes, cap, wide), ('x', 'z'), 0, 0, tiled=True)  35.1 us
    all_to_all x1, blocking collectives, body(): lax.all_to_all(partial.reshape(2 * lanes, 1, slot_count), ('core', 'x', '...  30 us
    ppermute x1, starting transfers between devices, body(): other = lax.ppermute(block, 'core', [(0, 1), (1, 0)])  9.27 us
    all_to_all x1, starting transfers between devices, body(): lax.all_to_all(copies, 'y', 0, 0, tiled=True).reshape(NY * slot_count, wide)  4.18 us
  transfers between devices with their start and end apart: 2, of which 1 were waited for; matrix products, arithmetic and copies ran while one was open for 0% of the time, Pallas kernels for 0%

profile of v5, /device:TPU:1, one launch (start us, length us, event | category | flops | bytes accessed | tf_op | source)
XLA Modules:
  0.0 83.9 jit_solution(3130389841917228768)
XLA Ops:
  0.0 1.4 %shard_map.37 = bf16[128,1152]{1,0:T(8,128)(2,1)S(1)} custom-call(s32[1]{0:T(128)} %bitcast.refs_0_.core_ref, bf16[64,1024]{1,0:T(8,128)(2,1)} %refs_1_.1, s32[1,64]{1,0:T(1,128)} %bitcast.12, s32[1,64]{1,0:T(1,128)} %bitcast.14), custom_call_target="tpu_custom_call" | custom-call | tf_op jit(solution)/shard_map/pallas_call | solution.py:148
  1.4 0.1 reshape.31
  1.6 35.1 %all_to_all.15 = bf16[64,2,1152]{2,1,0:T(2,128)(2,1)S(1)} all-to-all(bf16[64,2,1152]{2,1,0:T(2,128)(2,1)S(1)} %reshape.31), channel_id=1, replica_groups=mesh['y'=4,'core'=2,'x'=4,'z'=16] {'x','z'}, dimensions={0} | all-to-all | bytes 589824 | tf_op jit(solution)/shard_map/all_to_all | solution.py:159
  36.7 0.1 reshape.32.own_ref
  36.8 1.1 %broadcast_in_dim.2 = bf16[4,128,1152]{2,1,0:T(8,128)(2,1)} broadcast(bf16[128,1152]{1,0:T(8,128)(2,1)S(1)} %reshape.32.own_ref), dimensions={1,2} | broadcast | bytes 1474560 | tf_op jit(solution)/shard_map/broadcast_in_dim | solution.py:163
  37.9 4.2 %all-to-all-start.1 = ((bf16[4,128,1152]{2,1,0:T(8,128)(2,1)}), bf16[4,128,1152]{2,1,0:T(8,128)(2,1)S(1)}, u32[]{:S(2)}, u32[]{:S(2)}) async-start(bf16[4,128,1152]{2,1,0:T(8,128)(2,1)} %broadcast_in_dim.2), calls=%async_computation.1 | async-start | bytes 2359296 | tf_op jit(solution)/shard_map/all_to_all | solution.py:164
  42.1 0.0 copy-start
  42.1 9.3 %collective-permute-start = (bf16[128,1152]{1,0:T(8,128)(2,1)S(1)}, bf16[128,1152]{1,0:T(8,128)(2,1)S(1)}, u32[]{:S(2)}, u32[]{:S(2)}) collective-permute-start(bf16[128,1152]{1,0:T(8,128)(2,1)S(1)} %reshape.32.own_ref), channel_id=1, source_target_pairs={{0,64},{64,0},{1,65},{65,1},{2,66},{66,2},{3,67},{67,3},{4,68},{68... | collective-permute-start | bytes 884744 | tf_op jit(solution)/shard_map/ppermute | solution.py:162
  51.4 1.2 %collective-permute-done.other_ref = bf16[128,1152]{1,0:T(8,128)(2,1)S(1)} collective-permute-done((bf16[128,1152]{1,0:T(8,128)(2,1)S(1)}, bf16[128,1152]{1,0:T(8,128)(2,1)S(1)}, u32[]{:S(2)}, u32[]{:S(2)}) %collective-permute-start) | collective-permute-done | bytes 294944 | tf_op jit(solution)/shard_map/ppermute | solution.py:162
  52.6 0.0 all-to-all-done.1
  52.6 0.7 shard_map.38
  53.3 30.0 %all_to_all.16 = f32[128,1,128]{2,1,0:T(1,128)S(1)} all-to-all(f32[128,1,128]{2,1,0:T(1,128)S(1)} %bitcast.10), channel_id=1, replica_groups=mesh['y'=4,'core'=2,'x'=4,'z'=16] {'core','x','z'}, dimensions={0} | all-to-all | bytes 131072 | tf_op jit(solution)/shard_map/all_to_all | solution.py:170
  83.3 0.0 copy-done
  83.3 0.7 shard_map.39
Async XLA Ops:
  37.9 14.7 %all-to-all-start.1 = ((bf16[4,128,1152]{2,1,0:T(8,128)(2,1)}), bf16[4,128,1152]{2,1,0:T(8,128)(2,1)S(1)}, u32[]{:S(2)}, u32[]{:S(2)}) async-start(bf16[4,128,1152]{2,1,0:T(8,128)(2,1)} %broadcast_in_dim.2), calls=%async_computation.1 | async-start | bytes 2359296 | tf_op jit(solution)/shard_map/all_to_all | solution.py:164
  42.1 41.1 %copy-start = (s32[64]{0:T(128)S(1)}, s32[64]{0:T(128)}, u32[]{:S(2)}) copy-start(s32[64]{0:T(128)} %param.4) | copy-start | bytes 772
  42.1 10.5 %collective-permute-start = (bf16[128,1152]{1,0:T(8,128)(2,1)S(1)}, bf16[128,1152]{1,0:T(8,128)(2,1)S(1)}, u32[]{:S(2)}, u32[]{:S(2)}) collective-permute-start(bf16[128,1152]{1,0:T(8,128)(2,1)S(1)} %reshape.32.own_ref), channel_id=1, source_target_pairs={{0,64},{64,0},{1,65},{65,1},{2,66},{66,2},{3,67},{67,3},{4,68},{68... | collective-permute-start | bytes 884744 | tf_op jit(solution)/shard_map/ppermute | solution.py:162

commit v6 on v5

--- a/solution.py
+++ b/solution.py
@@ -8,7 +8,8 @@
 
 EPSILON = 1e-06
 DOWN, ACROSS = 4, 4
-SERIAL = 7
+SERIAL = 6
+SHIFTS = (3, 1, 2)
 NX = 4
 NY = 4
 META = 128
@@ -28,7 +29,7 @@
     return target, hit, place
 
 
-def pack_kernel(lanes, core_ref, emb_hbm, labels_hbm, order_hbm, out_ref, emb_ref, labels_ref, order_ref, arrived):
+def pack_kernel(lanes, core_ref, emb_hbm, labels_hbm, order_hbm, out_ref, slot_ref, emb_ref, labels_ref, order_ref, arrived):
     rows, width = emb_ref.shape
     tall, wide = rows // DOWN, width // ACROSS
     pieces = [(pl.ds(r * tall, tall), pl.ds(c * wide, wide)) for r in range(DOWN) for c in range(ACROSS)]
@@ -57,7 +58,9 @@
     labels, order = labels_ref[...], order_ref[...]
     target, _, place = slots(labels, lanes)
     cap = slot_count // lanes
-    here = lax.broadcasted_iota(jnp.int32, (slot_count, rows), 0) == target * cap + place
+    slot = target * cap + place
+    slot_ref[...] = slot
+    here = lax.broadcasted_iota(jnp.int32, (slot_count, rows), 0) == slot
 
     def column(values):
         return jnp.sum(jnp.where(here, values.astype(jnp.float32), 0.0), axis=1, keepdims=True)
@@ -84,13 +87,14 @@
     ).astype(jnp.bfloat16)
 
 
-def gram_kernel(core_ref, own_ref, other_ref, lane_ref, out_ref):
+def gram_kernel(core_ref, own_ref, other_ref, *rest):
+    lane_refs, out_ref = rest[:-1], rest[-1]
     width = own_ref.shape[1] - META
     size = own_ref.shape[0]
     dests = out_ref.shape[0] // 2
     core = core_ref[0]
     queries = jnp.concatenate([own_ref[...], other_ref[...]], axis=0)
-    members = lane_ref[...]
+    members = jnp.concatenate([own_ref[...]] + [ref[...] for ref in lane_refs], axis=0)
     scores = lax.dot_general(
         members[:, :width], queries[:, :width], NT, preferred_element_type=jnp.float32
     )
@@ -112,16 +116,17 @@
     out_ref[dests:, :] = jnp.where(mine, jnp.where(core == 0, other, own), -4.0)
 
 
-def pick_kernel(returned_ref, labels_ref, out_ref):
+def pick_kernel(returned_ref, slot_ref, out_ref):
     lanes, size = returned_ref.shape[0] // 2, returned_ref.shape[1]
-    _, hit, place = slots(labels_ref[...], lanes)
     cap = size // lanes
+    slot = slot_ref[...]
+    owner = lax.broadcasted_iota(jnp.int32, (lanes, slot.shape[1]), 0) * cap
     lane = lax.rem(lax.broadcasted_iota(jnp.int32, (lanes, size), 1), cap)
     returned = jnp.maximum(returned_ref[:lanes, :], returned_ref[lanes:, :])
-    best = jnp.full(hit.shape, -4.0, jnp.float32)
+    best = jnp.full(owner.shape, -4.0, jnp.float32)
     for p in range(cap):
         value = jnp.max(jnp.where(lane == p, returned, -4.0), axis=1, keepdims=True)
-        best = jnp.where(hit & (place == p), value, best)
+        best = jnp.where(slot == owner + p, value, best)
     out_ref[...] = jnp.max(best, axis=0, keepdims=True)
 
 
@@ -145,9 +150,12 @@
     labels, order = labels.reshape(1, rows), order.reshape(1, rows)
 
     core = lax.axis_index("core").astype(jnp.int32).reshape(1)
-    sent = call(
+    sent, slot = call(
         lambda *refs: pack_kernel(lanes, *refs),
-        jax.ShapeDtypeStruct((slot_count, wide), jnp.bfloat16),
+        [
+            jax.ShapeDtypeStruct((slot_count, wide), jnp.bfloat16),
+            jax.ShapeDtypeStruct((1, rows), jnp.int32),
+        ],
         [pl.BlockSpec(memory_space=pltpu.SMEM)] + [pl.BlockSpec(memory_space=pltpu.HBM)] * 3,
         [
             pltpu.VMEM((rows, width), jnp.bfloat16),
@@ -159,19 +167,20 @@
     block = lax.all_to_all(sent.reshape(lanes, cap, wide), ("x", "z"), 0, 0, tiled=True)
     block = block.reshape(slot_count, wide)
 
+    lane = [
+        lax.ppermute(block, "y", [(y, (y + shift) % NY) for y in range(NY)]) for shift in SHIFTS
+    ]
     other = lax.ppermute(block, "core", [(0, 1), (1, 0)])
-    copies = jnp.broadcast_to(block[None], (NY, slot_count, wide))
-    lane = lax.all_to_all(copies, "y", 0, 0, tiled=True).reshape(NY * slot_count, wide)
     partial = call(
         gram_kernel,
         jax.ShapeDtypeStruct((2 * lanes, slot_count), jnp.float32),
-        [pl.BlockSpec(memory_space=pltpu.SMEM)] + [VMEM] * 3,
-    )(core, block, other, lane)
+        [pl.BlockSpec(memory_space=pltpu.SMEM)] + [VMEM] * (1 + NY),
+    )(core, block, other, *lane)
     returned = lax.all_to_all(
         partial.reshape(2 * lanes, 1, slot_count), ("core", "x", "z"), 0, 0, tiled=True
     )
     best = call(pick_kernel, jax.ShapeDtypeStruct((1, rows), jnp.float32), [VMEM] * 2)(
-        returned.reshape(2 * lanes, slot_count), labels
+        returned.reshape(2 * lanes, slot_count), slot
     )
     return best.reshape(rows)
 

time: 84.5 us -> 83.7 us (level)
  starting transfers between devices: 13.5 us -> 20.7 us
  blocking collectives: 65.1 us -> 58.2 us
  local copies, waits for them, and re-layouts: 1.33 us -> 0.22 us
    ppermute x0 -> x3, starting transfers between devices: none -> 11.3 us  [body(): lax.ppermute(block, 'y', [(y, (y + shift) % NY) for y in range(NY)])]
    all_to_all x1, blocking collectives: 30 us -> 22.8 us  [body(): lax.all_to_all(partial.reshape(2 * lanes, 1, slot_count), ('core', 'x', '...]
    all_to_all x1 -> x0, starting transfers between devices: 4.18 us -> none  [body(): lax.all_to_all(copies, 'y', 0, 0, tiled=True).reshape(NY * slot_count, wide)]
    broadcast_in_dim x1 -> x0, local copies, waits for them, and re-layouts: 1.1 us -> none  [body(): copies = jnp.broadcast_to(block[None], (NY, slot_count, wide))]
  transfers between devices with their start and end apart: 2 -> 4, of which waited for: 1 -> 1; matrix products, arithmetic and copies ran while one was open for 0% -> 0% of each run, Pallas kernels for 0% -> 0%
where the time goes in v6:
time: 83.7 us; the launch traced here: 83.1 us
  blocking collectives  58.2 us (70%)
  starting transfers between devices  20.7 us (25%)
  Pallas kernels  2.73 us (3%)
  waiting for transfers between devices  1.16 us (1%)
    all_to_all x1, blocking collectives, body(): lax.all_to_all(sent.reshape(lanes, cap, wide), ('x', 'z'), 0, 0, tiled=True)  35.3 us
    all_to_all x1, blocking collectives, body(): lax.all_to_all(partial.reshape(2 * lanes, 1, slot_count), ('core', 'x', '...  22.8 us
    ppermute x3, starting transfers between devices, body(): lax.ppermute(block, 'y', [(y, (y + shift) % NY) for y in range(NY)])  11.3 us
    ppermute x1, starting transfers between devices, body(): other = lax.ppermute(block, 'core', [(0, 1), (1, 0)])  9.42 us
  transfers between devices with their start and end apart: 4, of which 1 were waited for; matrix products, arithmetic and copies ran while one was open for 0% of the time, Pallas kernels for 0%

profile of v6, /device:TPU:1, one launch (start us, length us, event | category | flops | bytes accessed | tf_op | source)
XLA Modules:
  0.0 83.1 jit_solution(1034428197221572904)
XLA Ops:
  0.0 1.4 %shard_map.37 = (bf16[128,1152]{1,0:T(8,128)(2,1)S(1)}, s32[1,64]{1,0:T(1,128)S(1)}) custom-call(s32[1]{0:T(128)} %bitcast.refs_0_.core_ref, bf16[64,1024]{1,0:T(8,128)(2,1)} %refs_1_.1, s32[1,64]{1,0:T(1,128)} %bitcast.10, s32[1,64]{1,0:T(1,128)} %bitcast.11), custom_call_target="tpu_custom_call" | custom-call | tf_op jit(solution)/shard_map/pallas_call | solution.py:153
  1.4 0.1 reshape.27
  1.6 35.3 %all_to_all.10 = bf16[64,2,1152]{2,1,0:T(2,128)(2,1)S(1)} all-to-all(bf16[64,2,1152]{2,1,0:T(2,128)(2,1)S(1)} %reshape.27), channel_id=1, replica_groups=mesh['y'=4,'core'=2,'x'=4,'z'=16] {'x','z'}, dimensions={0} | all-to-all | bytes 589824 | tf_op jit(solution)/shard_map/all_to_all | solution.py:167
  36.9 0.1 reshape.28.own_ref
  37.0 4.8 %collective-permute-start.3 = (bf16[128,1152]{1,0:T(8,128)(2,1)S(1)}, bf16[128,1152]{1,0:T(8,128)(2,1)S(1)}, u32[]{:S(2)}, u32[]{:S(2)}) collective-permute-start(bf16[128,1152]{1,0:T(8,128)(2,1)S(1)} %reshape.28.own_ref), channel_id=1, source_target_pairs={{0,256},{128,384},{256,0},{384,128},{1,257},{129,385},{257,1},{385... | collective-permute-start | bytes 884744 | tf_op jit(solution)/shard_map/ppermute | solution.py:171
  41.9 2.3 %collective-permute-start.2 = (bf16[128,1152]{1,0:T(8,128)(2,1)S(1)}, bf16[128,1152]{1,0:T(8,128)(2,1)S(1)}, u32[]{:S(2)}, u32[]{:S(2)}) collective-permute-start(bf16[128,1152]{1,0:T(8,128)(2,1)S(1)} %reshape.28.own_ref), channel_id=1, source_target_pairs={{0,128},{128,256},{256,384},{384,0},{1,129},{129,257},{257,385},{3... | collective-permute-start | bytes 884744 | tf_op jit(solution)/shard_map/ppermute | solution.py:171
  44.2 4.2 %collective-permute-start.1 = (bf16[128,1152]{1,0:T(8,128)(2,1)S(1)}, bf16[128,1152]{1,0:T(8,128)(2,1)S(1)}, u32[]{:S(2)}, u32[]{:S(2)}) collective-permute-start(bf16[128,1152]{1,0:T(8,128)(2,1)S(1)} %reshape.28.own_ref), channel_id=1, source_target_pairs={{0,384},{128,0},{256,128},{384,256},{1,385},{129,1},{257,129},{385... | collective-permute-start | bytes 884744 | tf_op jit(solution)/shard_map/ppermute | solution.py:171
  48.4 9.4 %collective-permute-start = (bf16[128,1152]{1,0:T(8,128)(2,1)S(1)}, bf16[128,1152]{1,0:T(8,128)(2,1)S(1)}, u32[]{:S(2)}, u32[]{:S(2)}) collective-permute-start(bf16[128,1152]{1,0:T(8,128)(2,1)S(1)} %reshape.28.own_ref), channel_id=1, source_target_pairs={{0,64},{64,0},{1,65},{65,1},{2,66},{66,2},{3,67},{67,3},{4,68},{68... | collective-permute-start | bytes 884744 | tf_op jit(solution)/shard_map/ppermute | solution.py:173
  57.8 0.0 collective-permute-done.3.rest_2_
  57.8 0.0 collective-permute-done.2.rest_1_
  57.8 0.0 collective-permute-done.1.rest_0_
  57.8 1.2 %collective-permute-done.other_ref = bf16[128,1152]{1,0:T(8,128)(2,1)S(1)} collective-permute-done((bf16[128,1152]{1,0:T(8,128)(2,1)S(1)}, bf16[128,1152]{1,0:T(8,128)(2,1)S(1)}, u32[]{:S(2)}, u32[]{:S(2)}) %collective-permute-start) | collective-permute-done | bytes 294944 | tf_op jit(solution)/shard_map/ppermute | solution.py:173
  59.0 0.7 shard_map.38
  59.7 22.8 %all_to_all.11 = f32[128,1,128]{2,1,0:T(1,128)S(1)} all-to-all(f32[128,1,128]{2,1,0:T(1,128)S(1)} %bitcast.8), channel_id=1, replica_groups=mesh['y'=4,'core'=2,'x'=4,'z'=16] {'core','x','z'}, dimensions={0} | all-to-all | bytes 131072 | tf_op jit(solution)/shard_map/all_to_all | solution.py:179
  82.5 0.6 shard_map.39
Async XLA Ops:
  37.0 20.8 %collective-permute-start.3 = (bf16[128,1152]{1,0:T(8,128)(2,1)S(1)}, bf16[128,1152]{1,0:T(8,128)(2,1)S(1)}, u32[]{:S(2)}, u32[]{:S(2)}) collective-permute-start(bf16[128,1152]{1,0:T(8,128)(2,1)S(1)} %reshape.28.own_ref), channel_id=1, source_target_pairs={{0,256},{128,384},{256,0},{384,128},{1,257},{129,385},{257,1},{385... | collective-permute-start | bytes 884744 | tf_op jit(solution)/shard_map/ppermute | solution.py:171
  41.9 16.0 %collective-permute-start.2 = (bf16[128,1152]{1,0:T(8,128)(2,1)S(1)}, bf16[128,1152]{1,0:T(8,128)(2,1)S(1)}, u32[]{:S(2)}, u32[]{:S(2)}) collective-permute-start(bf16[128,1152]{1,0:T(8,128)(2,1)S(1)} %reshape.28.own_ref), channel_id=1, source_target_pairs={{0,128},{128,256},{256,384},{384,0},{1,129},{129,257},{257,385},{3... | collective-permute-start | bytes 884744 | tf_op jit(solution)/shard_map/ppermute | solution.py:171
  44.2 13.7 %collective-permute-start.1 = (bf16[128,1152]{1,0:T(8,128)(2,1)S(1)}, bf16[128,1152]{1,0:T(8,128)(2,1)S(1)}, u32[]{:S(2)}, u32[]{:S(2)}) collective-permute-start(bf16[128,1152]{1,0:T(8,128)(2,1)S(1)} %reshape.28.own_ref), channel_id=1, source_target_pairs={{0,384},{128,0},{256,128},{384,256},{1,385},{129,1},{257,129},{385... | collective-permute-start | bytes 884744 | tf_op jit(solution)/shard_map/ppermute | solution.py:171
  48.4 10.6 %collective-permute-start = (bf16[128,1152]{1,0:T(8,128)(2,1)S(1)}, bf16[128,1152]{1,0:T(8,128)(2,1)S(1)}, u32[]{:S(2)}, u32[]{:S(2)}) collective-permute-start(bf16[128,1152]{1,0:T(8,128)(2,1)S(1)} %reshape.28.own_ref), channel_id=1, source_target_pairs={{0,64},{64,0},{1,65},{65,1},{2,66},{66,2},{3,67},{67,3},{4,68},{68... | collective-permute-start | bytes 884744 | tf_op jit(solution)/shard_map/ppermute | solution.py:173

commit v7 on v6

--- a/solution.py
+++ b/solution.py
@@ -87,14 +87,9 @@
     ).astype(jnp.bfloat16)
 
 
-def gram_kernel(core_ref, own_ref, other_ref, *rest):
-    lane_refs, out_ref = rest[:-1], rest[-1]
-    width = own_ref.shape[1] - META
-    size = own_ref.shape[0]
-    dests = out_ref.shape[0] // 2
-    core = core_ref[0]
-    queries = jnp.concatenate([own_ref[...], other_ref[...]], axis=0)
-    members = jnp.concatenate([own_ref[...]] + [ref[...] for ref in lane_refs], axis=0)
+def best_of(queries, member_refs):
+    width = queries.shape[1] - META
+    members = jnp.concatenate([ref[...] for ref in member_refs], axis=0)
     scores = lax.dot_general(
         members[:, :width], queries[:, :width], NT, preferred_element_type=jnp.float32
     )
@@ -107,8 +102,20 @@
     label_down = down[:, 0:1]
     order_down = down[:, 1:2] * 256.0 + down[:, 2:3]
     valid = (label_down == across[0:1, :]) & (order_down < across[1:2, :])
-    best = jnp.max(jnp.where(valid, scores, -1.0), axis=0, keepdims=True)
-    own, other = best[:, :size], best[:, size:]
+    return jnp.max(jnp.where(valid, scores, -1.0), axis=0, keepdims=True)
+
+
+def early_kernel(own_ref, *rest):
+    rest[-1][...] = best_of(own_ref[...], (own_ref, *rest[:-1]))
+
+
+def late_kernel(core_ref, early_ref, own_ref, other_ref, last_ref, *rest):
+    lane_refs, out_ref = rest[:-1], rest[-1]
+    size = own_ref.shape[0]
+    dests = out_ref.shape[0] // 2
+    core = core_ref[0]
+    own = jnp.maximum(early_ref[...], best_of(own_ref[...], (last_ref,)))
+    other = best_of(other_ref[...], (own_ref, last_ref, *lane_refs))
     home = lax.broadcasted_iota(jnp.int32, (dests, size), 0)
     slot = lax.broadcasted_iota(jnp.int32, (dests, size), 1) // (size // dests)
     mine = home == slot
@@ -171,11 +178,15 @@
         lax.ppermute(block, "y", [(y, (y + shift) % NY) for y in range(NY)]) for shift in SHIFTS
     ]
     other = lax.ppermute(block, "core", [(0, 1), (1, 0)])
+    last, ready = lane[0], [lane[1], lane[2]]
+    early = call(early_kernel, jax.ShapeDtypeStruct((1, slot_count), jnp.float32), [VMEM] * 3)(
+        block, *ready
+    )
     partial = call(
-        gram_kernel,
+        late_kernel,
         jax.ShapeDtypeStruct((2 * lanes, slot_count), jnp.float32),
-        [pl.BlockSpec(memory_space=pltpu.SMEM)] + [VMEM] * (1 + NY),
-    )(core, block, other, *lane)
+        [pl.BlockSpec(memory_space=pltpu.SMEM)] + [VMEM] * 6,
+    )(core, early, block, other, last, *ready)
     returned = lax.all_to_all(
         partial.reshape(2 * lanes, 1, slot_count), ("core", "x", "z"), 0, 0, tiled=True
     )

time: 83.7 us -> 83.6 us (level)
  transfers between devices with their start and end apart: 4 -> 4, of which waited for: 1 -> 1; matrix products, arithmetic and copies ran while one was open for 0% -> 0% of each run, Pallas kernels for 0% -> 1%
where the time goes in v7:
time: 83.6 us; the launch traced here: 83 us
  blocking collectives  58.2 us (70%)
  starting transfers between devices  20.7 us (25%)
  Pallas kernels  3.13 us (4%)
    all_to_all x1, blocking collectives, body(): lax.all_to_all(sent.reshape(lanes, cap, wide), ('x', 'z'), 0, 0, tiled=True)  35.3 us
    all_to_all x1, blocking collectives, body(): lax.all_to_all(partial.reshape(2 * lanes, 1, slot_count), ('core', 'x', '...  22.8 us
    ppermute x3, starting transfers between devices, body(): lax.ppermute(block, 'y', [(y, (y + shift) % NY) for y in range(NY)])  11.3 us
    ppermute x1, starting transfers between devices, body(): other = lax.ppermute(block, 'core', [(0, 1), (1, 0)])  9.42 us
  transfers between devices with their start and end apart: 4, of which 1 were waited for; matrix products, arithmetic and copies ran while one was open for 0% of the time, Pallas kernels for 1%

profile of v7, /device:TPU:1, one launch (start us, length us, event | category | flops | bytes accessed | tf_op | source)
XLA Modules:
  0.0 83.0 jit_solution(2036235020188698723)
XLA Ops:
  0.0 1.4 %shard_map.37 = (bf16[128,1152]{1,0:T(8,128)(2,1)S(1)}, s32[1,64]{1,0:T(1,128)S(1)}) custom-call(s32[1]{0:T(128)} %bitcast.refs_0_.core_ref, bf16[64,1024]{1,0:T(8,128)(2,1)} %refs_1_.1, s32[1,64]{1,0:T(1,128)} %bitcast.10, s32[1,64]{1,0:T(1,128)} %bitcast.11), custom_call_target="tpu_custom_call" | custom-call | tf_op jit(solution)/shard_map/pallas_call | solution.py:160
  1.4 0.1 reshape.27
  1.6 35.3 %all_to_all.10 = bf16[64,2,1152]{2,1,0:T(2,128)(2,1)S(1)} all-to-all(bf16[64,2,1152]{2,1,0:T(2,128)(2,1)S(1)} %reshape.27), channel_id=1, replica_groups=mesh['y'=4,'core'=2,'x'=4,'z'=16] {'x','z'}, dimensions={0} | all-to-all | bytes 589824 | tf_op jit(solution)/shard_map/all_to_all | solution.py:174
  36.9 0.1 reshape.28.own_ref
  37.0 4.8 %collective-permute-start.1 = (bf16[128,1152]{1,0:T(8,128)(2,1)S(1)}, bf16[128,1152]{1,0:T(8,128)(2,1)S(1)}, u32[]{:S(2)}, u32[]{:S(2)}) collective-permute-start(bf16[128,1152]{1,0:T(8,128)(2,1)S(1)} %reshape.28.own_ref), channel_id=1, source_target_pairs={{0,256},{128,384},{256,0},{384,128},{1,257},{129,385},{257,1},{385... | collective-permute-start | bytes 884744 | tf_op jit(solution)/shard_map/ppermute | solution.py:178
  41.9 2.3 %collective-permute-start = (bf16[128,1152]{1,0:T(8,128)(2,1)S(1)}, bf16[128,1152]{1,0:T(8,128)(2,1)S(1)}, u32[]{:S(2)}, u32[]{:S(2)}) collective-permute-start(bf16[128,1152]{1,0:T(8,128)(2,1)S(1)} %reshape.28.own_ref), channel_id=1, source_target_pairs={{0,128},{128,256},{256,384},{384,0},{1,129},{129,257},{257,385},{3... | collective-permute-start | bytes 884744 | tf_op jit(solution)/shard_map/ppermute | solution.py:178
  44.2 4.2 %collective-permute-start.3 = (bf16[128,1152]{1,0:T(8,128)(2,1)S(1)}, bf16[128,1152]{1,0:T(8,128)(2,1)S(1)}, u32[]{:S(2)}, u32[]{:S(2)}) collective-permute-start(bf16[128,1152]{1,0:T(8,128)(2,1)S(1)} %reshape.28.own_ref), channel_id=1, source_target_pairs={{0,384},{128,0},{256,128},{384,256},{1,385},{129,1},{257,129},{385... | collective-permute-start | bytes 884744 | tf_op jit(solution)/shard_map/ppermute | solution.py:178
  48.4 9.4 %collective-permute-start.2 = (bf16[128,1152]{1,0:T(8,128)(2,1)S(1)}, bf16[128,1152]{1,0:T(8,128)(2,1)S(1)}, u32[]{:S(2)}, u32[]{:S(2)}) collective-permute-start(bf16[128,1152]{1,0:T(8,128)(2,1)S(1)} %reshape.28.own_ref), channel_id=1, source_target_pairs={{0,64},{64,0},{1,65},{65,1},{2,66},{66,2},{3,67},{67,3},{4,68},{68... | collective-permute-start | bytes 884744 | tf_op jit(solution)/shard_map/ppermute | solution.py:180
  57.8 0.0 collective-permute-done.1.rest_1_
  57.8 0.0 collective-permute-done.rest_0_
  57.8 0.5 shard_map.38.early_ref
  58.3 0.0 collective-permute-done.3.last_ref
  58.3 0.7 collective-permute-done.2.other_ref
  59.0 0.6 shard_map.39
  59.6 22.8 %all_to_all.11 = f32[128,1,128]{2,1,0:T(1,128)S(1)} all-to-all(f32[128,1,128]{2,1,0:T(1,128)S(1)} %bitcast.9), channel_id=1, replica_groups=mesh['y'=4,'core'=2,'x'=4,'z'=16] {'core','x','z'}, dimensions={0} | all-to-all | bytes 131072 | tf_op jit(solution)/shard_map/all_to_all | solution.py:190
  82.4 0.6 shard_map.40
Async XLA Ops:
  37.0 20.8 %collective-permute-start.1 = (bf16[128,1152]{1,0:T(8,128)(2,1)S(1)}, bf16[128,1152]{1,0:T(8,128)(2,1)S(1)}, u32[]{:S(2)}, u32[]{:S(2)}) collective-permute-start(bf16[128,1152]{1,0:T(8,128)(2,1)S(1)} %reshape.28.own_ref), channel_id=1, source_target_pairs={{0,256},{128,384},{256,0},{384,128},{1,257},{129,385},{257,1},{385... | collective-permute-start | bytes 884744 | tf_op jit(solution)/shard_map/ppermute | solution.py:178
  41.9 16.0 %collective-permute-start = (bf16[128,1152]{1,0:T(8,128)(2,1)S(1)}, bf16[128,1152]{1,0:T(8,128)(2,1)S(1)}, u32[]{:S(2)}, u32[]{:S(2)}) collective-permute-start(bf16[128,1152]{1,0:T(8,128)(2,1)S(1)} %reshape.28.own_ref), channel_id=1, source_target_pairs={{0,128},{128,256},{256,384},{384,0},{1,129},{129,257},{257,385},{3... | collective-permute-start | bytes 884744 | tf_op jit(solution)/shard_map/ppermute | solution.py:178
  44.2 14.1 %collective-permute-start.3 = (bf16[128,1152]{1,0:T(8,128)(2,1)S(1)}, bf16[128,1152]{1,0:T(8,128)(2,1)S(1)}, u32[]{:S(2)}, u32[]{:S(2)}) collective-permute-start(bf16[128,1152]{1,0:T(8,128)(2,1)S(1)} %reshape.28.own_ref), channel_id=1, source_target_pairs={{0,384},{128,0},{256,128},{384,256},{1,385},{129,1},{257,129},{385... | collective-permute-start | bytes 884744 | tf_op jit(solution)/shard_map/ppermute | solution.py:178
  48.4 10.6 %collective-permute-start.2 = (bf16[128,1152]{1,0:T(8,128)(2,1)S(1)}, bf16[128,1152]{1,0:T(8,128)(2,1)S(1)}, u32[]{:S(2)}, u32[]{:S(2)}) collective-permute-start(bf16[128,1152]{1,0:T(8,128)(2,1)S(1)} %reshape.28.own_ref), channel_id=1, source_target_pairs={{0,64},{64,0},{1,65},{65,1},{2,66},{66,2},{3,67},{67,3},{4,68},{68... | collective-permute-start | bytes 884744 | tf_op jit(solution)/shard_map/ppermute | solution.py:180

commit v8 on v7

--- a/solution.py
+++ b/solution.py
@@ -58,8 +58,9 @@
     labels, order = labels_ref[...], order_ref[...]
     target, _, place = slots(labels, lanes)
     cap = slot_count // lanes
-    slot = target * cap + place
-    slot_ref[...] = slot
+    slot_ref[...] = target * cap + place
+    nz = lanes // NX
+    slot = (lax.rem(target, nz) * NX + target // nz) * cap + place
     here = lax.broadcasted_iota(jnp.int32, (slot_count, rows), 0) == slot
 
     def column(values):
@@ -118,6 +119,7 @@
     other = best_of(other_ref[...], (own_ref, last_ref, *lane_refs))
     home = lax.broadcasted_iota(jnp.int32, (dests, size), 0)
     slot = lax.broadcasted_iota(jnp.int32, (dests, size), 1) // (size // dests)
+    slot = lax.rem(slot, NX) * (dests // NX) + slot // NX
     mine = home == slot
     out_ref[:dests, :] = jnp.where(mine, jnp.where(core == 0, own, other), -4.0)
     out_ref[dests:, :] = jnp.where(mine, jnp.where(core == 0, other, own), -4.0)
@@ -171,7 +173,7 @@
             pltpu.SemaphoreType.DMA((2 + DOWN * ACROSS,)),
         ],
     )(core, *[pltpu.with_memory_space_constraint(a, pltpu.HBM) for a in (embeddings, labels, order)])
-    block = lax.all_to_all(sent.reshape(lanes, cap, wide), ("x", "z"), 0, 0, tiled=True)
+    block = lax.all_to_all(sent.reshape(lanes, cap, wide), ("z", "x"), 0, 0, tiled=True)
     block = block.reshape(slot_count, wide)
 
     lane = [

time: 83.6 us -> 83.6 us (level)
    all_to_all x1, blocking collectives: 22.8 us -> 20.9 us  [body(): lax.all_to_all(partial.reshape(2 * lanes, 1, slot_count), ('core', 'x', '...]
    all_to_all x1, blocking collectives: 35.3 us -> 37 us  [body(): lax.all_to_all(sent.reshape(lanes, cap, wide), ('z', 'x'), 0, 0, tiled=True)]
where the time goes in v8:
time: 83.6 us; the launch traced here: 83 us
  blocking collectives  57.9 us (69%)
  starting transfers between devices  21 us (25%)
  Pallas kernels  3.14 us (4%)
    all_to_all x1, blocking collectives, body(): lax.all_to_all(sent.reshape(lanes, cap, wide), ('z', 'x'), 0, 0, tiled=True)  37 us
    all_to_all x1, blocking collectives, body(): lax.all_to_all(partial.reshape(2 * lanes, 1, slot_count), ('core', 'x', '...  20.9 us
    ppermute x3, starting transfers between devices, body(): lax.ppermute(block, 'y', [(y, (y + shift) % NY) for y in range(NY)])  11.3 us
    ppermute x1, starting transfers between devices, body(): other = lax.ppermute(block, 'core', [(0, 1), (1, 0)])  9.66 us
  transfers between devices with their start and end apart: 4, of which 1 were waited for; matrix products, arithmetic and copies ran while one was open for 0% of the time, Pallas kernels for 1%

profile of v8, /device:TPU:1, one launch (start us, length us, event | category | flops | bytes accessed | tf_op | source)
XLA Modules:
  0.0 83.0 jit_solution(7432027477640144441)
XLA Ops:
  0.0 1.4 %shard_map.37 = (bf16[128,1152]{1,0:T(8,128)(2,1)S(1)}, s32[1,64]{1,0:T(1,128)S(1)}) custom-call(s32[1]{0:T(128)} %bitcast.refs_0_.core_ref, bf16[64,1024]{1,0:T(8,128)(2,1)} %refs_1_.1, s32[1,64]{1,0:T(1,128)} %bitcast.10, s32[1,64]{1,0:T(1,128)} %bitcast.11), custom_call_target="tpu_custom_call" | custom-call | tf_op jit(solution)/shard_map/pallas_call | solution.py:162
  1.4 0.1 reshape.27
  1.6 37.0 %all_to_all.10 = bf16[64,2,1152]{2,1,0:T(2,128)(2,1)S(1)} all-to-all(bf16[64,2,1152]{2,1,0:T(2,128)(2,1)S(1)} %reshape.27), channel_id=1, replica_groups=mesh['y'=4,'core'=2,'x'=4,'z'=16] {'z','x'}, dimensions={0} | all-to-all | bytes 589824 | tf_op jit(solution)/shard_map/all_to_all | solution.py:176
  38.5 0.1 reshape.28.own_ref
  38.6 4.8 %collective-permute-start.1 = (bf16[128,1152]{1,0:T(8,128)(2,1)S(1)}, bf16[128,1152]{1,0:T(8,128)(2,1)S(1)}, u32[]{:S(2)}, u32[]{:S(2)}) collective-permute-start(bf16[128,1152]{1,0:T(8,128)(2,1)S(1)} %reshape.28.own_ref), channel_id=1, source_target_pairs={{0,256},{128,384},{256,0},{384,128},{1,257},{129,385},{257,1},{385... | collective-permute-start | bytes 884744 | tf_op jit(solution)/shard_map/ppermute | solution.py:180
  43.5 2.3 %collective-permute-start = (bf16[128,1152]{1,0:T(8,128)(2,1)S(1)}, bf16[128,1152]{1,0:T(8,128)(2,1)S(1)}, u32[]{:S(2)}, u32[]{:S(2)}) collective-permute-start(bf16[128,1152]{1,0:T(8,128)(2,1)S(1)} %reshape.28.own_ref), channel_id=1, source_target_pairs={{0,128},{128,256},{256,384},{384,0},{1,129},{129,257},{257,385},{3... | collective-permute-start | bytes 884744 | tf_op jit(solution)/shard_map/ppermute | solution.py:180
  45.8 4.2 %collective-permute-start.3 = (bf16[128,1152]{1,0:T(8,128)(2,1)S(1)}, bf16[128,1152]{1,0:T(8,128)(2,1)S(1)}, u32[]{:S(2)}, u32[]{:S(2)}) collective-permute-start(bf16[128,1152]{1,0:T(8,128)(2,1)S(1)} %reshape.28.own_ref), channel_id=1, source_target_pairs={{0,384},{128,0},{256,128},{384,256},{1,385},{129,1},{257,129},{385... | collective-permute-start | bytes 884744 | tf_op jit(solution)/shard_map/ppermute | solution.py:180
  50.0 9.7 %collective-permute-start.2 = (bf16[128,1152]{1,0:T(8,128)(2,1)S(1)}, bf16[128,1152]{1,0:T(8,128)(2,1)S(1)}, u32[]{:S(2)}, u32[]{:S(2)}) collective-permute-start(bf16[128,1152]{1,0:T(8,128)(2,1)S(1)} %reshape.28.own_ref), channel_id=1, source_target_pairs={{0,64},{64,0},{1,65},{65,1},{2,66},{66,2},{3,67},{67,3},{4,68},{68... | collective-permute-start | bytes 884744 | tf_op jit(solution)/shard_map/ppermute | solution.py:182
  59.6 0.0 collective-permute-done.1.rest_1_
  59.7 0.0 collective-permute-done.rest_0_
  59.7 0.5 shard_map.38.early_ref
  60.1 0.0 collective-permute-done.3.last_ref
  60.1 0.7 collective-permute-done.2.other_ref
  60.8 0.6 shard_map.39
  61.5 20.9 %all_to_all.11 = f32[128,1,128]{2,1,0:T(1,128)S(1)} all-to-all(f32[128,1,128]{2,1,0:T(1,128)S(1)} %bitcast.9), channel_id=1, replica_groups=mesh['y'=4,'core'=2,'x'=4,'z'=16] {'core','x','z'}, dimensions={0} | all-to-all | bytes 131072 | tf_op jit(solution)/shard_map/all_to_all | solution.py:192
  82.4 0.6 shard_map.40
Async XLA Ops:
  38.6 21.0 %collective-permute-start.1 = (bf16[128,1152]{1,0:T(8,128)(2,1)S(1)}, bf16[128,1152]{1,0:T(8,128)(2,1)S(1)}, u32[]{:S(2)}, u32[]{:S(2)}) collective-permute-start(bf16[128,1152]{1,0:T(8,128)(2,1)S(1)} %reshape.28.own_ref), channel_id=1, source_target_pairs={{0,256},{128,384},{256,0},{384,128},{1,257},{129,385},{257,1},{385... | collective-permute-start | bytes 884744 | tf_op jit(solution)/shard_map/ppermute | solution.py:180
  43.5 16.2 %collective-permute-start = (bf16[128,1152]{1,0:T(8,128)(2,1)S(1)}, bf16[128,1152]{1,0:T(8,128)(2,1)S(1)}, u32[]{:S(2)}, u32[]{:S(2)}) collective-permute-start(bf16[128,1152]{1,0:T(8,128)(2,1)S(1)} %reshape.28.own_ref), channel_id=1, source_target_pairs={{0,128},{128,256},{256,384},{384,0},{1,129},{129,257},{257,385},{3... | collective-permute-start | bytes 884744 | tf_op jit(solution)/shard_map/ppermute | solution.py:180
  45.8 14.3 %collective-permute-start.3 = (bf16[128,1152]{1,0:T(8,128)(2,1)S(1)}, bf16[128,1152]{1,0:T(8,128)(2,1)S(1)}, u32[]{:S(2)}, u32[]{:S(2)}) collective-permute-start(bf16[128,1152]{1,0:T(8,128)(2,1)S(1)} %reshape.28.own_ref), channel_id=1, source_target_pairs={{0,384},{128,0},{256,128},{384,256},{1,385},{129,1},{257,129},{385... | collective-permute-start | bytes 884744 | tf_op jit(solution)/shard_map/ppermute | solution.py:180
  50.0 10.9 %collective-permute-start.2 = (bf16[128,1152]{1,0:T(8,128)(2,1)S(1)}, bf16[128,1152]{1,0:T(8,128)(2,1)S(1)}, u32[]{:S(2)}, u32[]{:S(2)}) collective-permute-start(bf16[128,1152]{1,0:T(8,128)(2,1)S(1)} %reshape.28.own_ref), channel_id=1, source_target_pairs={{0,64},{64,0},{1,65},{65,1},{2,66},{66,2},{3,67},{67,3},{4,68},{68... | collective-permute-start | bytes 884744 | tf_op jit(solution)/shard_map/ppermute | solution.py:182
